TPU v7x, 512 devices: a whole 4x4x16 slice. The times are simulated.
512 devices in a mesh: rep: 16 (over x_hi, y, core), fsdp: 32 (over z, x_lo).
Axes of the slice: x: 4 (x_hi: 2, x_lo: 2; x = x_hi * 2 + x_lo), y: 4, z: 16, core: 2. Of those that a mesh axis runs over, the one named last changes fastest.
Arguments:
- weights: bfloat16 [6, 6144, 1024], P(None, 'fsdp'), may hold values from -0.078125 to 0.078125
- momentum: bfloat16 [6144, 1024], P('fsdp'), may hold values from -0.023925781 to 0.023925781
- pseudo_grad: bfloat16 [16, 6144, 1024], P('rep', 'fsdp'), may hold values from -0.078125 to 0.078125
- tokens: bfloat16 [65536, 6144], P(('rep', 'fsdp')), may hold values from -6 to 6
- fragment: int32 [6], replicated, may hold values from 0 to 5, each once
Outputs:
- new_weights: bfloat16 [16, 6144, 1024], P('rep', 'fsdp')
- new_momentum: bfloat16 [6144, 1024], P('fsdp')
- layer_out: bfloat16 [65536, 1024], P(('rep', 'fsdp'))
Inputs may be any that keep to these rules, and one draw needn't show every extreme that they name: fragment holds each of the 6 layer indices once.
All inputs are finite; a program needn't handle non-finite values.
Results may differ from a plain program's by a relative error of at most 0.017.
Values may be sent and summed in bfloat16 or wider, within the bound.
No kernel may reach another device: no remote copies, remote signals or barrier semaphores. Data moves between devices by JAX's collectives and lax.ppermute only.
A program may use at most 64 MiB of HBM per device.

v0:
```python
import jax
import jax.numpy as jnp
from jax import lax
from jax.sharding import PartitionSpec as P

MU = 0.9
OUTER_LR = 0.7
MIX = 0.5


def per_device(weights, momentum, pseudo_grad, tokens, fragment):
    index = fragment[0]
    second = fragment[1]
    synced = lax.dynamic_index_in_dim(weights, index, 0, keepdims=False)
    following = lax.dynamic_index_in_dim(weights, second, 0, keepdims=False)
    product = jnp.dot(
        tokens,
        lax.all_gather(following, "fsdp", axis=0, tiled=True),
        preferred_element_type=jnp.float32,
    )
    layer_out = product.astype(jnp.bfloat16)
    replicas = lax.axis_size("rep")
    own_grad = pseudo_grad[0].astype(jnp.float32)
    averaged = lax.psum(own_grad.astype(jnp.bfloat16), "rep").astype(jnp.float32) / replicas
    velocity = MU * momentum.astype(jnp.float32) + averaged
    synced_wide = synced.astype(jnp.float32)
    outer_weights = synced_wide - OUTER_LR * (averaged + MU * velocity)
    inner_weights = synced_wide - own_grad
    blended = (MIX * inner_weights + (1.0 - MIX) * outer_weights).astype(jnp.bfloat16)
    return (blended[None], velocity.astype(jnp.bfloat16), layer_out)


def solution(mesh):
    in_specs = (
        P(None, "fsdp", None),
        P("fsdp", None),
        P("rep", "fsdp", None),
        P(("rep", "fsdp"), None),
        P(),
    )
    out_specs = (P("rep", "fsdp", None), P("fsdp", None), P(("rep", "fsdp"), None))
    return jax.shard_map(
        per_device, mesh=mesh, in_specs=in_specs, out_specs=out_specs, check_vma=False
    )
```

profile of v0, /device:TPU:59, one launch (start us, length us, event | category | flops | bytes accessed | tf_op | source)
XLA Modules:
  0.0 345.5 jit_solution(13102914976574267197)
XLA Ops:
  8.0 0.0 copy-start
  8.0 0.0 all-reduce.2.cloned.1.call-start
  8.1 0.7 all-reduce.2.cloned.1.call-update
  8.7 0.0 all-gather.3.cloned.1.call-start
  8.8 1.3 fusion.13
  12.1 1.8 constant_dynamic-slice_fusion
  13.9 0.0 all-gather.3.cloned.1.call-update
  15.9 312.3 %all-reduce.2.cloned.1.call-done = bf16[192,1024]{1,0:T(8,128)(2,1)} async-done(((bf16[192,1024]{1,0:T(8,128)(2,1)}), bf16[192,1024]{1,0:T(8,128)(2,1)}) %all-reduce.2.cloned.1.call-update) | async-done | bytes 393232 | tf_op jit(solution)/shard_map/psum | solution.py:24
  328.1 2.6 fusion.11
  330.8 0.0 all-gather.3.cloned.1.call-done
  330.8 0.0 copy-done
  330.8 6.5 %fusion.5 = bf16[128,1024]{0,1:T(8,128)(2,1)S(1)} fusion(bf16[128,6144]{1,0:T(8,128)(2,1)S(1)} %copy-done, bf16[1,6144,1024]{2,1,0:T(8,128)(2,1)} %all-gather.3.cloned.1.call-done), kind=kOutput, calls=%fused_computation.3 | convolution fusion | flops 1610743808 | bytes 14417920 | tf_op jit(solution)/shard_map/dot_general | solution.py:16
  337.2 0.9 copy.8
Async XLA Ops:
  8.0 322.8 %copy-start = (bf16[128,6144]{1,0:T(8,128)(2,1)S(1)}, bf16[128,6144]{1,0:T(8,128)(2,1)}, u32[]{:S(2)}) copy-start(bf16[128,6144]{1,0:T(8,128)(2,1)} %param.8) | copy-start | bytes 4718596
  8.0 320.1 %all-reduce.2.cloned.1.call-start = ((), (), s32[]{:S(2)}) async-start(), calls=%async_computation | async-start | bytes 786432 | tf_op jit(solution)/shard_map/psum | solution.py:24
  8.7 322.0 %all-gather.3.cloned.1.call-start = ((), (), s32[]{:S(2)}) async-start(), calls=%async_computation.1 | async-start | bytes 12976128 | tf_op jit(solution)/shard_map/all_gather | solution.py:18
Sparse Core Ops, SparseCore 0:
  11.7 316.3 all-reduce.1
Sparse Core Ops, SparseCore 1:
  14.0 290.2 all-gather.2
where the time goes:
time: 346 us
  waiting for transfers between devices  313 us (90%)
  between operations  19.4 us (6%)
  matrix products  6.46 us (2%)
  local copies, waits for them, and re-layouts  4.01 us (1%)
    psum x1, waiting for transfers between devices, per_device(): lax.psum(own_grad.astype(jnp.bfloat16), 'rep').astype(jnp.float32)  312 us
  transfers between devices with their start and end apart: 2, of which 1 were waited for; matrix products, arithmetic and copies ran while one was open for 2% of the time, Pallas kernels for 0%

commit v1 on v0

v1 whole, which is shorter than its diff:
```python
import jax
import jax.numpy as jnp
from jax import lax
from jax.experimental import pallas as pl
from jax.experimental.pallas import tpu as pltpu
from jax.sharding import Mesh, PartitionSpec as P

MU = 0.9
OUTER_LR = 0.7
MIX = 0.5

SIZES = {"xh": 2, "y": 4, "core": 2, "zh": 4, "zl": 4, "xl": 2}
AXES = tuple(SIZES)
REP = ("xh", "y", "core")
FSDP = ("zh", "zl", "xl")
CHIPS = 4
PARTS = 4

ANY = pl.BlockSpec(memory_space=pl.ANY)


def permute(value, move):
    pairs = []
    total = 1
    for size in SIZES.values():
        total *= size
    for source in range(total):
        rest, at = source, {}
        for axis in reversed(AXES):
            at[axis] = rest % SIZES[axis]
            rest //= SIZES[axis]
        to = move(dict(at))
        target = 0
        for axis in AXES:
            target = target * SIZES[axis] + to[axis] % SIZES[axis]
        pairs.append((source, target))
    return lax.ppermute(value, AXES, pairs)


def along_z(step):
    def move(at):
        z = (at["zh"] * SIZES["zl"] + at["zl"] + step) % (SIZES["zh"] * SIZES["zl"])
        at["zh"], at["zl"] = divmod(z, SIZES["zl"])
        return at

    return move


def in_group(step):
    def move(at):
        if at["core"] == 0:
            at["y"] = (at["y"] + step) % SIZES["y"]
        else:
            x = (at["xh"] * SIZES["xl"] + at["xl"] + step) % (SIZES["xh"] * SIZES["xl"])
            at["xh"], at["xl"] = divmod(x, SIZES["xl"])
        return at

    return move


def flip(axis, bit=1):
    def move(at):
        at[axis] ^= bit
        return at

    return move


def quarter(xl):
    return lax.rem(lax.axis_index("xh") * SIZES["xl"] + xl + lax.axis_index("y"), CHIPS)


def pick(weights, fragment):
    rows, cols = weights.shape[1:]
    width = cols // (CHIPS * SIZES["core"])

    def kernel(fragment_ref, weights_ref, own_ref, give_ref, sems):
        xl = lax.axis_index("xl")
        core = lax.axis_index("core")
        copies = []
        for n, (ref, at) in enumerate(((own_ref, xl), (give_ref, 1 - xl))):
            start = pl.multiple_of((quarter(at) * SIZES["core"] + core) * width, 128)
            source = weights_ref.at[fragment_ref[1], :, pl.ds(start, width)]
            copies.append(pltpu.make_async_copy(source, ref, sems.at[n]))
        for copy in copies:
            copy.start()
        for copy in copies:
            copy.wait()

    shape = jax.ShapeDtypeStruct((rows, width), weights.dtype)
    return pl.pallas_call(
        kernel,
        out_shape=(shape, shape),
        in_specs=[pl.BlockSpec(memory_space=pltpu.SMEM), ANY],
        out_specs=(ANY, ANY),
        scratch_shapes=[pltpu.SemaphoreType.DMA((2,))],
    )(fragment, weights)


def multiply(blocks, own, other):
    tokens, depth = blocks[0].shape
    places, steps, rows, width = own.shape

    def kernel(*refs):
        token_refs, (own_ref, other_ref) = refs[:CHIPS], refs[CHIPS : CHIPS + 2]
        out_refs, total = refs[CHIPS + 2 : -1], refs[-1]
        zl, core = lax.axis_index("zl"), lax.axis_index("core")
        step = pl.program_id(0)

        @pl.when(step == 0)
        def _():
            total[...] = jnp.zeros_like(total)

        for n, token_ref in enumerate(token_refs):
            part = None
            for place in range(places):
                weight = jnp.concatenate([own_ref[place, 0], other_ref[place, 0]], axis=1)
                start = pl.multiple_of(lax.rem(zl + place, places) * rows, 128)
                term = jnp.dot(
                    token_ref[:, pl.ds(start, rows)], weight, preferred_element_type=jnp.float32
                )
                part = term if part is None else part + term
            total[n] += part

        @pl.when(step == steps - 1)
        def _():
            mine = pl.multiple_of(core * width, 128)
            theirs = pl.multiple_of((1 - core) * width, 128)
            for n, out_ref in enumerate(out_refs):
                out_ref[:, pl.ds(mine, width)] = total[n, :, :width].astype(out_ref.dtype)
                out_ref[:, pl.ds(theirs, width)] = total[n, :, width:].astype(out_ref.dtype)

    weight_spec = pl.BlockSpec((places, 1, rows, width), lambda s: (0, s, 0, 0))
    shape = jax.ShapeDtypeStruct((tokens, 2 * width), blocks[0].dtype)
    return pl.pallas_call(
        kernel,
        grid=(steps,),
        out_shape=(shape,) * CHIPS,
        in_specs=[pl.BlockSpec((tokens, depth // steps), lambda s: (0, s))] * CHIPS + [weight_spec] * 2,
        out_specs=(pl.BlockSpec((tokens, 2 * width), lambda s: (0, 0)),) * CHIPS,
        scratch_shapes=[pltpu.VMEM((CHIPS, tokens, 2 * width), jnp.float32)],
        compiler_params=pltpu.CompilerParams(vmem_limit_bytes=32 << 20),
        cost_estimate=pl.CostEstimate(
            flops=2 * CHIPS * tokens * depth * 2 * width,
            bytes_accessed=2 * (CHIPS * tokens * depth + depth * 2 * width),
            transcendentals=0,
        ),
    )(*blocks, own, other)


def assemble(results):
    tokens, width = results[0].shape

    def kernel(*refs):
        out_ref = refs[-1]
        first = quarter(lax.axis_index("xl"))
        for n, ref in enumerate(refs[:-1]):
            start = pl.multiple_of(lax.rem(first + n, CHIPS) * width, 128)
            out_ref[:, pl.ds(start, width)] = ref[...]

    return pl.pallas_call(
        kernel,
        out_shape=jax.ShapeDtypeStruct((tokens, CHIPS * width), results[0].dtype),
        in_specs=[pl.BlockSpec(memory_space=pltpu.VMEM)] * CHIPS,
        out_specs=pl.BlockSpec(memory_space=pltpu.VMEM),
    )(*results)


def ordered(first, mine, other):
    return jnp.where(first, jnp.concatenate([mine, other]), jnp.concatenate([other, mine]))


def layer_product(weights, tokens, fragment):
    own, give = pick(weights, fragment)
    partner = permute(give, flip("xl"))
    blocks = [tokens] + [permute(tokens, in_group(step)) for step in (1, 2, 3)]
    plane = ordered(lax.axis_index("xl") == 0, own, partner)
    here = lax.all_gather(plane, "zh", axis=0, tiled=True)
    half = here.shape[0] // 2
    before = permute(here, along_z(1))
    after = permute(here, along_z(-1))
    far_low = permute(before[:half], along_z(1))
    far_high = permute(after[half:], along_z(-1))
    held = jnp.concatenate([here, after, far_low, far_high, before])
    other = permute(held, flip("core"))
    shape = (SIZES["zl"], SIZES["zh"], *plane.shape)
    outs = multiply(blocks, held.reshape(shape), other.reshape(shape))
    results = [outs[0]] + [permute(outs[step], in_group(-step)) for step in (1, 2, 3)]
    return assemble(results)


def sum_over_rep(grad):
    core = lax.axis_index("core")
    half = grad.shape[0] // 2
    mine = lax.dynamic_slice_in_dim(grad, core * half, half)
    theirs = lax.dynamic_slice_in_dim(grad, (1 - core) * half, half)

    def add(a, b):
        return (a.astype(jnp.float32) + b.astype(jnp.float32)).astype(grad.dtype)

    total = add(mine, permute(theirs, flip("core")))
    for move in (flip("xh"), flip("y"), flip("y", 2)):
        total = add(total, permute(total, move))
    return ordered(core == 0, total, permute(total, flip("core")))


def per_device(weights, momentum, pseudo_grad, tokens, fragment):
    layer_out = layer_product(weights, tokens, fragment)
    synced = lax.dynamic_index_in_dim(weights, fragment[0], 0, keepdims=False)
    replicas = lax.axis_size(REP)
    own_grad = pseudo_grad[0].astype(jnp.float32)
    averaged = sum_over_rep(pseudo_grad[0]).astype(jnp.float32) / replicas
    velocity = MU * momentum.astype(jnp.float32) + averaged
    synced_wide = synced.astype(jnp.float32)
    outer_weights = synced_wide - OUTER_LR * (averaged + MU * velocity)
    inner_weights = synced_wide - own_grad
    blended = (MIX * inner_weights + (1.0 - MIX) * outer_weights).astype(jnp.bfloat16)
    return (blended[None], velocity.astype(jnp.bfloat16), layer_out)


def solution(mesh):
    split = Mesh(mesh.devices.reshape(tuple(SIZES.values())), AXES)
    in_specs = (
        P(None, FSDP, None),
        P(FSDP, None),
        P(REP, FSDP, None),
        P(REP + FSDP, None),
        P(),
    )
    out_specs = (P(REP, FSDP, None), P(FSDP, None), P(REP + FSDP, None))
    return jax.shard_map(
        per_device, mesh=split, in_specs=in_specs, out_specs=out_specs, check_vma=False
    )
```

time: 346 us -> 132 us (0.38)
  the two profiles are of different devices: /device:TPU:59 before, /device:TPU:4 now
where the time goes in v1:
time: 132 us; the launch traced here: 131 us
  starting transfers between devices  55.9 us (42%)
  blocking collectives  29.1 us (22%)
  waiting for transfers between devices  24.2 us (18%)
  Pallas kernels  12 us (9%)
  local copies, waits for them, and re-layouts  5.4 us (4%)
  other arithmetic  3.42 us (3%)
    ppermute x17, starting transfers between devices, permute(): return lax.ppermute(value, AXES, pairs)  55.9 us
    all_gather x1, blocking collectives, layer_product(): here = lax.all_gather(plane, 'zh', axis=0, tiled=True)  29.1 us
    ppermute x17, waiting for transfers between devices, permute(): return lax.ppermute(value, AXES, pairs)  24.2 us
    pallas_call x1, Pallas kernels, multiply(): pl.pallas_call(kernel, grid=(steps,), out_shape=(shape,) * CHIPS, in_spec...  5.44 us
    pallas_call x1, Pallas kernels, pick(): pl.pallas_call(kernel, out_shape=(shape, shape), in_specs=[pl.BlockSpec(m...  4.91 us
  transfers between devices with their start and end apart: 17, of which 6 were waited for; matrix products, arithmetic and copies ran while one was open for 5% of the time, Pallas kernels for 4%

profile of v1, /device:TPU:4, one launch (start us, length us, event | category | flops | bytes accessed | tf_op | source)
XLA Modules:
  0.0 131.2 jit_solution(4236961826211681288)
XLA Ops:
  0.7 4.9 %shard_map.76 = (bf16[192,128]{1,0:T(8,128)(2,1)}, bf16[192,128]{1,0:T(8,128)(2,1)}) custom-call(s32[6]{0:T(128)} %fragment_ref.1, bf16[6,192,1024]{2,1,0:T(8,128)(2,1)} %weights_ref.1), custom_call_target="tpu_custom_call" | custom-call | tf_op jit(solution)/shard_map/pallas_call | solution.py:91
  5.6 3.1 %collective-permute-start.8 = (bf16[192,128]{1,0:T(8,128)(2,1)}, bf16[192,128]{1,0:T(8,128)(2,1)S(1)}, u32[]{:S(2)}, u32[]{:S(2)}) collective-permute-start(bf16[192,128]{1,0:T(8,128)(2,1)} %get-tuple-element.10), channel_id=1, source_target_pairs={{0,1},{1,0},{2,3},{3,2},{4,5},{5,4},{6,7},{7,6},{8,9},{9,8},{10,11... | collective-permute-start | bytes 147464 | tf_op jit(solution)/shard_map/ppermute | solution.py:37
  8.7 3.1 %collective-permute-done.8 = bf16[192,128]{1,0:T(8,128)(2,1)S(1)} collective-permute-done((bf16[192,128]{1,0:T(8,128)(2,1)}, bf16[192,128]{1,0:T(8,128)(2,1)S(1)}, u32[]{:S(2)}, u32[]{:S(2)}) %collective-permute-start.8) | collective-permute-done | bytes 49184 | tf_op jit(solution)/shard_map/ppermute | solution.py:37
  12.7 29.1 %all_gather.3 = bf16[1536,128]{1,0:T(8,128)(2,1)S(1)} all-gather(bf16[384,128]{1,0:T(8,128)(2,1)S(1)} %maximum_select_fusion.1), channel_id=1, replica_groups=mesh['xh'=2,'y'=4,'core'=2,'zh'=4,'zl'=4,'xl'=2] {'zh'}, dimensions={0}, use_global_device_ids=true | all-gather | bytes 491520 | tf_op jit(solution)/shard_map/all_gather | solution.py:178
  43.6 5.1 %collective-permute-start.9 = (bf16[1536,128]{1,0:T(8,128)(2,1)S(1)}, bf16[1536,128]{1,0:T(8,128)(2,1)}, u32[]{:S(2)}, u32[]{:S(2)}) collective-permute-start(bf16[1536,128]{1,0:T(8,128)(2,1)S(1)} %all_gather.3), channel_id=1, source_target_pairs={{0,30},{1,31},{2,0},{3,1},{4,2},{5,3},{6,4},{7,5},{8,6},{9,7},{10,... | collective-permute-start | bytes 1179656 | tf_op jit(solution)/shard_map/ppermute | solution.py:37
  48.8 3.5 %collective-permute-start.5 = (bf16[128,6144]{1,0:T(8,128)(2,1)S(1)}, bf16[128,6144]{1,0:T(8,128)(2,1)}, u32[]{:S(2)}, u32[]{:S(2)}) collective-permute-start(bf16[128,6144]{1,0:T(8,128)(2,1)S(1)} %copy-done), channel_id=1, source_target_pairs={{0,64},{1,65},{2,66},{3,67},{4,68},{5,69},{6,70},{7,71},{8,72},{9,... | collective-permute-start | bytes 4718600 | tf_op jit(solution)/shard_map/ppermute | solution.py:37
  52.3 4.8 %collective-permute-start.6 = (bf16[128,6144]{1,0:T(8,128)(2,1)S(1)}, bf16[128,6144]{1,0:T(8,128)(2,1)}, u32[]{:S(2)}, u32[]{:S(2)}) collective-permute-start(bf16[128,6144]{1,0:T(8,128)(2,1)S(1)} %copy-done), channel_id=1, source_target_pairs={{0,128},{1,129},{2,130},{3,131},{4,132},{5,133},{6,134},{7,135},{8... | collective-permute-start | bytes 4718600 | tf_op jit(solution)/shard_map/ppermute | solution.py:37
  57.1 3.3 %collective-permute-start.7 = (bf16[128,6144]{1,0:T(8,128)(2,1)S(1)}, bf16[128,6144]{1,0:T(8,128)(2,1)}, u32[]{:S(2)}, u32[]{:S(2)}) collective-permute-start(bf16[128,6144]{1,0:T(8,128)(2,1)S(1)} %copy-done), channel_id=1, source_target_pairs={{0,192},{1,193},{2,194},{3,195},{4,196},{5,197},{6,198},{7,199},{8... | collective-permute-start | bytes 4718600 | tf_op jit(solution)/shard_map/ppermute | solution.py:37
  61.5 1.9 %collective-permute-start.11 = (bf16[768,128]{1,0:T(8,128)(2,1)S(1)}, bf16[768,128]{1,0:T(8,128)(2,1)S(1)}, u32[]{:S(2)}, u32[]{:S(2)}) collective-permute-start(bf16[768,128]{1,0:T(8,128)(2,1)S(1)} %slice.12), channel_id=1, source_target_pairs={{0,2},{1,3},{2,4},{3,5},{4,6},{5,7},{6,8},{7,9},{8,10},{9,11},{10,... | collective-permute-start | bytes 589832 | tf_op jit(solution)/shard_map/ppermute | solution.py:37
  64.4 5.1 %collective-permute-start.12 = (bf16[768,128]{1,0:T(8,128)(2,1)S(1)}, bf16[768,128]{1,0:T(8,128)(2,1)S(1)}, u32[]{:S(2)}, u32[]{:S(2)}) collective-permute-start(bf16[768,128]{1,0:T(8,128)(2,1)S(1)} %slice.13), channel_id=1, source_target_pairs={{0,30},{1,31},{2,0},{3,1},{4,2},{5,3},{6,4},{7,5},{8,6},{9,7},{10,... | collective-permute-start | bytes 589832 | tf_op jit(solution)/shard_map/ppermute | solution.py:37
  70.6 1.9 %collective-permute-start = (bf16[96,1024]{1,0:T(8,128)(2,1)S(1)}, bf16[96,1024]{1,0:T(8,128)(2,1)S(1)}, u32[]{:S(2)}, u32[]{:S(2)}) collective-permute-start(bf16[96,1024]{1,0:T(8,128)(2,1)S(1)} %dynamic-slice_bitcast_fusion), channel_id=1, source_target_pairs={{0,32},{1,33},{2,34},{3,35},{4,36},{5,37},{6,38},{7,39},{8,40},{9,... | collective-permute-start | bytes 589832 | tf_op jit(solution)/shard_map/ppermute | solution.py:37
  73.8 2.3 %collective-permute-start.13 = (bf16[6144,128]{1,0:T(8,128)(2,1)S(1)}, bf16[6144,128]{1,0:T(8,128)(2,1)}, u32[]{:S(2)}, u32[]{:S(2)}) collective-permute-start(bf16[6144,128]{1,0:T(8,128)(2,1)S(1)} %constant_dynamic-update-slice_fusion), channel_id=1, source_target_pairs={{0,32},{1,33},{2,34},{3,35},{4,36},{5,37},{6,38},{7,39},{8,40},{9,... | collective-permute-start | bytes 4718600 | tf_op jit(solution)/shard_map/ppermute | solution.py:37
  76.1 2.4 %collective-permute-start.1 = (bf16[96,1024]{1,0:T(8,128)(2,1)S(1)}, bf16[96,1024]{1,0:T(8,128)(2,1)S(1)}, u32[]{:S(2)}, u32[]{:S(2)}) collective-permute-start(bf16[96,1024]{1,0:T(8,128)(2,1)S(1)} %fusion.4), channel_id=1, source_target_pairs={{0,256},{1,257},{2,258},{3,259},{4,260},{5,261},{6,262},{7,263},{8... | collective-permute-start | bytes 589832 | tf_op jit(solution)/shard_map/ppermute | solution.py:37
  78.6 8.3 %collective-permute-done.1 = bf16[96,1024]{1,0:T(8,128)(2,1)S(1)} collective-permute-done((bf16[96,1024]{1,0:T(8,128)(2,1)S(1)}, bf16[96,1024]{1,0:T(8,128)(2,1)S(1)}, u32[]{:S(2)}, u32[]{:S(2)}) %collective-permute-start.1) | collective-permute-done | bytes 196640 | tf_op jit(solution)/shard_map/ppermute | solution.py:37
  86.9 3.2 %collective-permute-start.2 = (bf16[96,1024]{1,0:T(8,128)(2,1)S(1)}, bf16[96,1024]{1,0:T(8,128)(2,1)S(1)}, u32[]{:S(2)}, u32[]{:S(2)}) collective-permute-start(bf16[96,1024]{1,0:T(8,128)(2,1)S(1)} %add_convert_fusion.2), channel_id=1, source_target_pairs={{0,64},{1,65},{2,66},{3,67},{4,68},{5,69},{6,70},{7,71},{8,72},{9,... | collective-permute-start | bytes 589832 | tf_op jit(solution)/shard_map/ppermute | solution.py:37
  90.1 6.2 %collective-permute-done.2 = bf16[96,1024]{1,0:T(8,128)(2,1)S(1)} collective-permute-done((bf16[96,1024]{1,0:T(8,128)(2,1)S(1)}, bf16[96,1024]{1,0:T(8,128)(2,1)S(1)}, u32[]{:S(2)}, u32[]{:S(2)}) %collective-permute-start.2) | collective-permute-done | bytes 196640 | tf_op jit(solution)/shard_map/ppermute | solution.py:37
  96.3 5.1 %collective-permute-start.3 = (bf16[96,1024]{1,0:T(8,128)(2,1)S(1)}, bf16[96,1024]{1,0:T(8,128)(2,1)S(1)}, u32[]{:S(2)}, u32[]{:S(2)}) collective-permute-start(bf16[96,1024]{1,0:T(8,128)(2,1)S(1)} %add_convert_fusion.1), channel_id=1, source_target_pairs={{0,128},{1,129},{2,130},{3,131},{4,132},{5,133},{6,134},{7,135},{8... | collective-permute-start | bytes 589832 | tf_op jit(solution)/shard_map/ppermute | solution.py:37
  101.4 4.8 %collective-permute-done.3 = bf16[96,1024]{1,0:T(8,128)(2,1)S(1)} collective-permute-done((bf16[96,1024]{1,0:T(8,128)(2,1)S(1)}, bf16[96,1024]{1,0:T(8,128)(2,1)S(1)}, u32[]{:S(2)}, u32[]{:S(2)}) %collective-permute-start.3) | collective-permute-done | bytes 196640 | tf_op jit(solution)/shard_map/ppermute | solution.py:37
  106.2 1.9 %collective-permute-start.4 = (bf16[96,1024]{1,0:T(8,128)(2,1)S(1)}, bf16[96,1024]{1,0:T(8,128)(2,1)S(1)}, u32[]{:S(2)}, u32[]{:S(2)}) collective-permute-start(bf16[96,1024]{1,0:T(8,128)(2,1)S(1)} %add_convert_fusion), channel_id=1, source_target_pairs={{0,32},{1,33},{2,34},{3,35},{4,36},{5,37},{6,38},{7,39},{8,40},{9,... | collective-permute-start | bytes 589832 | tf_op jit(solution)/shard_map/ppermute | solution.py:37
  108.3 5.4 %shard_map.77 = (bf16[128,256]{1,0:T(8,128)(2,1)S(1)}, bf16[128,256]{1,0:T(8,128)(2,1)S(1)}, bf16[128,256]{1,0:T(8,128)(2,1)S(1)}, bf16[128,256]{1,0:T(8,128)(2,1)S(1)}) custom-call(bf16[128,6144]{1,0:T(8,128)(2,1)S(1)} %copy-done, bf16[128,6144]{1,0:T(8,128)(2,1)} %collective-permute-done.5.refs_1_, bf16[128,6144]{1,0:T(8,128)(2,1)} %collective-permute-done.6.refs_2_, ...), custom_call_target="tpu_custom_call" | custom-call | flops 1610612736 | bytes 9437184 | tf_op jit(solution)/shard_map/pallas_call | solution.py:135
  114.4 3.2 %collective-permute-start.14 = (bf16[128,256]{1,0:T(8,128)(2,1)S(1)}, bf16[128,256]{1,0:T(8,128)(2,1)S(1)}, u32[]{:S(2)}, u32[]{:S(2)}) collective-permute-start(bf16[128,256]{1,0:T(8,128)(2,1)S(1)} %get-tuple-element.12), channel_id=1, source_target_pairs={{0,192},{1,193},{2,194},{3,195},{4,196},{5,197},{6,198},{7,199},{8... | collective-permute-start | bytes 196616 | tf_op jit(solution)/shard_map/ppermute | solution.py:37
  117.6 3.8 %collective-permute-start.15 = (bf16[128,256]{1,0:T(8,128)(2,1)S(1)}, bf16[128,256]{1,0:T(8,128)(2,1)S(1)}, u32[]{:S(2)}, u32[]{:S(2)}) collective-permute-start(bf16[128,256]{1,0:T(8,128)(2,1)S(1)} %get-tuple-element.13), channel_id=1, source_target_pairs={{0,128},{1,129},{2,130},{3,131},{4,132},{5,133},{6,134},{7,135},{8... | collective-permute-start | bytes 196616 | tf_op jit(solution)/shard_map/ppermute | solution.py:37
  121.5 3.3 %collective-permute-start.16 = (bf16[128,256]{1,0:T(8,128)(2,1)S(1)}, bf16[128,256]{1,0:T(8,128)(2,1)S(1)}, u32[]{:S(2)}, u32[]{:S(2)}) collective-permute-start(bf16[128,256]{1,0:T(8,128)(2,1)S(1)} %get-tuple-element.14), channel_id=1, source_target_pairs={{0,64},{1,65},{2,66},{3,67},{4,68},{5,69},{6,70},{7,71},{8,72},{9,... | collective-permute-start | bytes 196616 | tf_op jit(solution)/shard_map/ppermute | solution.py:37
  124.8 2.3 %fusion.3 = (bf16[192,1024]{1,0:T(8,128)(2,1)}, bf16[1,192,1024]{2,1,0:T(8,128)(2,1)}) fusion(bf16[192,1024]{1,0:T(8,128)(2,1)S(1)} %copy-done.5, bf16[96,1024]{1,0:T(8,128)(2,1)S(1)} %add_convert_fusion, bf16[96,1024]{1,0:T(8,128)(2,1)S(1)} %collective-permute-done.4, pred[]{:T(512)S(6)} %eq.6, bf16[1,192,1024]{2,1,0:T(8,128)(2,1)S(1)} %copy-done.4, ...), kind=kLoop, calls=%fused_computation.6 | loop fusion | flops 4915200 | bytes 2359301 | tf_op jit(solution)/shard_map/convert_element_type | solution.py:218
  (48 shorter events, 11.9 us)
Async XLA Ops:
  0.6 48.2 %copy-start = (bf16[128,6144]{1,0:T(8,128)(2,1)S(1)}, bf16[128,6144]{1,0:T(8,128)(2,1)}, u32[]{:S(2)}) copy-start(bf16[128,6144]{1,0:T(8,128)(2,1)} %refs_0_.1) | copy-start | bytes 4718596
  0.6 59.7 %copy-start.2 = (bf16[1,192,1024]{2,1,0:T(8,128)(2,1)S(1)}, bf16[1,192,1024]{2,1,0:T(8,128)(2,1)}, u32[]{:S(2)}) copy-start(bf16[1,192,1024]{2,1,0:T(8,128)(2,1)} %param.7) | copy-start | bytes 1179652
  5.6 6.2 %collective-permute-start.8 = (bf16[192,128]{1,0:T(8,128)(2,1)}, bf16[192,128]{1,0:T(8,128)(2,1)S(1)}, u32[]{:S(2)}, u32[]{:S(2)}) collective-permute-start(bf16[192,128]{1,0:T(8,128)(2,1)} %get-tuple-element.10), channel_id=1, source_target_pairs={{0,1},{1,0},{2,3},{3,2},{4,5},{5,4},{6,7},{7,6},{8,9},{9,8},{10,11... | collective-permute-start | bytes 147464 | tf_op jit(solution)/shard_map/ppermute | solution.py:37
  41.7 18.7 %collective-permute-start.10 = (bf16[1536,128]{1,0:T(8,128)(2,1)S(1)}, bf16[1536,128]{1,0:T(8,128)(2,1)}, u32[]{:S(2)}, u32[]{:S(2)}) collective-permute-start(bf16[1536,128]{1,0:T(8,128)(2,1)S(1)} %all_gather.3), channel_id=1, source_target_pairs={{0,2},{1,3},{2,4},{3,5},{4,6},{5,7},{6,8},{7,9},{8,10},{9,11},{10,... | collective-permute-start | bytes 1179656 | tf_op jit(solution)/shard_map/ppermute | solution.py:37
  43.6 19.8 %collective-permute-start.9 = (bf16[1536,128]{1,0:T(8,128)(2,1)S(1)}, bf16[1536,128]{1,0:T(8,128)(2,1)}, u32[]{:S(2)}, u32[]{:S(2)}) collective-permute-start(bf16[1536,128]{1,0:T(8,128)(2,1)S(1)} %all_gather.3), channel_id=1, source_target_pairs={{0,30},{1,31},{2,0},{3,1},{4,2},{5,3},{6,4},{7,5},{8,6},{9,7},{10,... | collective-permute-start | bytes 1179656 | tf_op jit(solution)/shard_map/ppermute | solution.py:37
  48.8 59.5 %collective-permute-start.5 = (bf16[128,6144]{1,0:T(8,128)(2,1)S(1)}, bf16[128,6144]{1,0:T(8,128)(2,1)}, u32[]{:S(2)}, u32[]{:S(2)}) collective-permute-start(bf16[128,6144]{1,0:T(8,128)(2,1)S(1)} %copy-done), channel_id=1, source_target_pairs={{0,64},{1,65},{2,66},{3,67},{4,68},{5,69},{6,70},{7,71},{8,72},{9,... | collective-permute-start | bytes 4718600 | tf_op jit(solution)/shard_map/ppermute | solution.py:37
  52.3 56.0 %collective-permute-start.6 = (bf16[128,6144]{1,0:T(8,128)(2,1)S(1)}, bf16[128,6144]{1,0:T(8,128)(2,1)}, u32[]{:S(2)}, u32[]{:S(2)}) collective-permute-start(bf16[128,6144]{1,0:T(8,128)(2,1)S(1)} %copy-done), channel_id=1, source_target_pairs={{0,128},{1,129},{2,130},{3,131},{4,132},{5,133},{6,134},{7,135},{8... | collective-permute-start | bytes 4718600 | tf_op jit(solution)/shard_map/ppermute | solution.py:37
  57.1 51.2 %collective-permute-start.7 = (bf16[128,6144]{1,0:T(8,128)(2,1)S(1)}, bf16[128,6144]{1,0:T(8,128)(2,1)}, u32[]{:S(2)}, u32[]{:S(2)}) collective-permute-start(bf16[128,6144]{1,0:T(8,128)(2,1)S(1)} %copy-done), channel_id=1, source_target_pairs={{0,192},{1,193},{2,194},{3,195},{4,196},{5,197},{6,198},{7,199},{8... | collective-permute-start | bytes 4718600 | tf_op jit(solution)/shard_map/ppermute | solution.py:37
  60.5 15.6 %copy-start.3 = (bf16[1,192,1024]{2,1,0:T(8,128)(2,1)S(1)}, bf16[1,192,1024]{2,1,0:T(8,128)(2,1)}, u32[]{:S(2)}) copy-start(bf16[1,192,1024]{2,1,0:T(8,128)(2,1)} %param.7) | copy-start | bytes 1179652
  61.5 9.1 %collective-permute-start.11 = (bf16[768,128]{1,0:T(8,128)(2,1)S(1)}, bf16[768,128]{1,0:T(8,128)(2,1)S(1)}, u32[]{:S(2)}, u32[]{:S(2)}) collective-permute-start(bf16[768,128]{1,0:T(8,128)(2,1)S(1)} %slice.12), channel_id=1, source_target_pairs={{0,2},{1,3},{2,4},{3,5},{4,6},{5,7},{6,8},{7,9},{8,10},{9,11},{10,... | collective-permute-start | bytes 589832 | tf_op jit(solution)/shard_map/ppermute | solution.py:37
  64.4 8.3 %collective-permute-start.12 = (bf16[768,128]{1,0:T(8,128)(2,1)S(1)}, bf16[768,128]{1,0:T(8,128)(2,1)S(1)}, u32[]{:S(2)}, u32[]{:S(2)}) collective-permute-start(bf16[768,128]{1,0:T(8,128)(2,1)S(1)} %slice.13), channel_id=1, source_target_pairs={{0,30},{1,31},{2,0},{3,1},{4,2},{5,3},{6,4},{7,5},{8,6},{9,7},{10,... | collective-permute-start | bytes 589832 | tf_op jit(solution)/shard_map/ppermute | solution.py:37
  70.6 5.5 %collective-permute-start = (bf16[96,1024]{1,0:T(8,128)(2,1)S(1)}, bf16[96,1024]{1,0:T(8,128)(2,1)S(1)}, u32[]{:S(2)}, u32[]{:S(2)}) collective-permute-start(bf16[96,1024]{1,0:T(8,128)(2,1)S(1)} %dynamic-slice_bitcast_fusion), channel_id=1, source_target_pairs={{0,32},{1,33},{2,34},{3,35},{4,36},{5,37},{6,38},{7,39},{8,40},{9,... | collective-permute-start | bytes 589832 | tf_op jit(solution)/shard_map/ppermute | solution.py:37
  72.7 35.5 %copy-start.9 = (s32[6]{0:T(128)S(1)}, s32[6]{0:T(128)}, u32[]{:S(2)}) copy-start(s32[6]{0:T(128)} %fragment_ref.1) | copy-start | bytes 76
  73.8 34.6 %collective-permute-start.13 = (bf16[6144,128]{1,0:T(8,128)(2,1)S(1)}, bf16[6144,128]{1,0:T(8,128)(2,1)}, u32[]{:S(2)}, u32[]{:S(2)}) collective-permute-start(bf16[6144,128]{1,0:T(8,128)(2,1)S(1)} %constant_dynamic-update-slice_fusion), channel_id=1, source_target_pairs={{0,32},{1,33},{2,34},{3,35},{4,36},{5,37},{6,38},{7,39},{8,40},{9,... | collective-permute-start | bytes 4718600 | tf_op jit(solution)/shard_map/ppermute | solution.py:37
  76.1 10.7 %collective-permute-start.1 = (bf16[96,1024]{1,0:T(8,128)(2,1)S(1)}, bf16[96,1024]{1,0:T(8,128)(2,1)S(1)}, u32[]{:S(2)}, u32[]{:S(2)}) collective-permute-start(bf16[96,1024]{1,0:T(8,128)(2,1)S(1)} %fusion.4), channel_id=1, source_target_pairs={{0,256},{1,257},{2,258},{3,259},{4,260},{5,261},{6,262},{7,263},{8... | collective-permute-start | bytes 589832 | tf_op jit(solution)/shard_map/ppermute | solution.py:37
  86.9 9.3 %collective-permute-start.2 = (bf16[96,1024]{1,0:T(8,128)(2,1)S(1)}, bf16[96,1024]{1,0:T(8,128)(2,1)S(1)}, u32[]{:S(2)}, u32[]{:S(2)}) collective-permute-start(bf16[96,1024]{1,0:T(8,128)(2,1)S(1)} %add_convert_fusion.2), channel_id=1, source_target_pairs={{0,64},{1,65},{2,66},{3,67},{4,68},{5,69},{6,70},{7,71},{8,72},{9,... | collective-permute-start | bytes 589832 | tf_op jit(solution)/shard_map/ppermute | solution.py:37
  96.3 9.9 %collective-permute-start.3 = (bf16[96,1024]{1,0:T(8,128)(2,1)S(1)}, bf16[96,1024]{1,0:T(8,128)(2,1)S(1)}, u32[]{:S(2)}, u32[]{:S(2)}) collective-permute-start(bf16[96,1024]{1,0:T(8,128)(2,1)S(1)} %add_convert_fusion.1), channel_id=1, source_target_pairs={{0,128},{1,129},{2,130},{3,131},{4,132},{5,133},{6,134},{7,135},{8... | collective-permute-start | bytes 589832 | tf_op jit(solution)/shard_map/ppermute | solution.py:37
  106.2 18.6 %collective-permute-start.4 = (bf16[96,1024]{1,0:T(8,128)(2,1)S(1)}, bf16[96,1024]{1,0:T(8,128)(2,1)S(1)}, u32[]{:S(2)}, u32[]{:S(2)}) collective-permute-start(bf16[96,1024]{1,0:T(8,128)(2,1)S(1)} %add_convert_fusion), channel_id=1, source_target_pairs={{0,32},{1,33},{2,34},{3,35},{4,36},{5,37},{6,38},{7,39},{8,40},{9,... | collective-permute-start | bytes 589832 | tf_op jit(solution)/shard_map/ppermute | solution.py:37
  108.3 16.5 %copy-start.4 = (bf16[1,192,1024]{2,1,0:T(8,128)(2,1)S(1)}, bf16[1,192,1024]{2,1,0:T(8,128)(2,1)}, u32[]{:S(2)}) copy-start(bf16[1,192,1024]{2,1,0:T(8,128)(2,1)} %param.7) | copy-start | bytes 1179652
  108.3 16.5 %copy-start.5 = (bf16[192,1024]{1,0:T(8,128)(2,1)S(1)}, bf16[192,1024]{1,0:T(8,128)(2,1)}, u32[]{:S(2)}) copy-start(bf16[192,1024]{1,0:T(8,128)(2,1)} %param.6) | copy-start | bytes 1179652
  114.4 12.7 %collective-permute-start.14 = (bf16[128,256]{1,0:T(8,128)(2,1)S(1)}, bf16[128,256]{1,0:T(8,128)(2,1)S(1)}, u32[]{:S(2)}, u32[]{:S(2)}) collective-permute-start(bf16[128,256]{1,0:T(8,128)(2,1)S(1)} %get-tuple-element.12), channel_id=1, source_target_pairs={{0,192},{1,193},{2,194},{3,195},{4,196},{5,197},{6,198},{7,199},{8... | collective-permute-start | bytes 196616 | tf_op jit(solution)/shard_map/ppermute | solution.py:37
  117.6 9.5 %collective-permute-start.15 = (bf16[128,256]{1,0:T(8,128)(2,1)S(1)}, bf16[128,256]{1,0:T(8,128)(2,1)S(1)}, u32[]{:S(2)}, u32[]{:S(2)}) collective-permute-start(bf16[128,256]{1,0:T(8,128)(2,1)S(1)} %get-tuple-element.13), channel_id=1, source_target_pairs={{0,128},{1,129},{2,130},{3,131},{4,132},{5,133},{6,134},{7,135},{8... | collective-permute-start | bytes 196616 | tf_op jit(solution)/shard_map/ppermute | solution.py:37
  121.5 7.4 %collective-permute-start.16 = (bf16[128,256]{1,0:T(8,128)(2,1)S(1)}, bf16[128,256]{1,0:T(8,128)(2,1)S(1)}, u32[]{:S(2)}, u32[]{:S(2)}) collective-permute-start(bf16[128,256]{1,0:T(8,128)(2,1)S(1)} %get-tuple-element.14), channel_id=1, source_target_pairs={{0,64},{1,65},{2,66},{3,67},{4,68},{5,69},{6,70},{7,71},{8,72},{9,... | collective-permute-start | bytes 196616 | tf_op jit(solution)/shard_map/ppermute | solution.py:37
  127.1 1.7 %copy-start.6 = (bf16[128,256]{1,0:T(8,128)(2,1)}, bf16[128,256]{1,0:T(8,128)(2,1)S(1)}, u32[]{:S(2)}) copy-start(bf16[128,256]{1,0:T(8,128)(2,1)S(1)} %collective-permute-done.14.refs_1_) | copy-start | bytes 196612
  (3 other events, 2.9 us)

commit v2 on v1

v2 whole, which is shorter than its diff:
```python
import jax
import jax.numpy as jnp
from jax import lax
from jax.experimental import pallas as pl
from jax.experimental.pallas import tpu as pltpu
from jax.sharding import Mesh, PartitionSpec as P

MU = 0.9
OUTER_LR = 0.7
MIX = 0.5

SIZES = {"xh": 2, "y": 4, "core": 2, "zh": 4, "zl": 4, "xl": 2}
AXES = tuple(SIZES)
REP = ("xh", "y", "core")
FSDP = ("zh", "zl", "xl")
CHIPS = 4
PARTS = SIZES["zl"]

ANY = pl.BlockSpec(memory_space=pl.ANY)
WHOLE = pl.BlockSpec(memory_space=pltpu.VMEM)


def in_vmem(*values):
    return [pltpu.with_memory_space_constraint(value, pltpu.VMEM) for value in values]


def in_hbm(*values):
    return [pltpu.with_memory_space_constraint(value, pltpu.HBM) for value in values]


def vmem_like(shape, dtype=jnp.bfloat16):
    return pltpu.VMEM(shape, dtype)


SMALL = pltpu.CompilerParams(vmem_limit_bytes=1 << 20)


def permute(value, move):
    pairs = []
    total = 1
    for size in SIZES.values():
        total *= size
    for source in range(total):
        rest, at = source, {}
        for axis in reversed(AXES):
            at[axis] = rest % SIZES[axis]
            rest //= SIZES[axis]
        to = move(dict(at))
        target = 0
        for axis in AXES:
            target = target * SIZES[axis] + to[axis] % SIZES[axis]
        pairs.append((source, target))
    return lax.ppermute(value, AXES, pairs)


def along_z(step):
    def move(at):
        z = (at["zh"] * SIZES["zl"] + at["zl"] + step) % (SIZES["zh"] * SIZES["zl"])
        at["zh"], at["zl"] = divmod(z, SIZES["zl"])
        return at

    return move


def in_group(step):
    def move(at):
        if at["core"] == 0:
            at["y"] = (at["y"] + step) % SIZES["y"]
        else:
            x = (at["xh"] * SIZES["xl"] + at["xl"] + step) % (SIZES["xh"] * SIZES["xl"])
            at["xh"], at["xl"] = divmod(x, SIZES["xl"])
        return at

    return move


def flip(axis, bit=1):
    def move(at):
        at[axis] ^= bit
        return at

    return move


def quarter(xl):
    return lax.rem(lax.axis_index("xh") * SIZES["xl"] + xl + lax.axis_index("y"), CHIPS)


def pick(weights, fragment):
    rows, cols = weights.shape[1:]
    width = cols // (CHIPS * SIZES["core"])

    def kernel(fragment_ref, weights_ref, own_ref, give_ref, sems):
        xl = lax.axis_index("xl")
        core = lax.axis_index("core")
        copies = []
        for n, (ref, at) in enumerate(((own_ref, xl), (give_ref, 1 - xl))):
            start = pl.multiple_of((quarter(at) * SIZES["core"] + core) * width, 128)
            source = weights_ref.at[fragment_ref[1], :, pl.ds(start, width)]
            copies.append(pltpu.make_async_copy(source, ref, sems.at[n]))
        for copy in copies:
            copy.start()
        for copy in copies:
            copy.wait()

    return pl.pallas_call(
        kernel,
        out_shape=[vmem_like((rows, width))] * 2,
        in_specs=[pl.BlockSpec(memory_space=pltpu.SMEM), ANY],
        out_specs=[WHOLE] * 2,
        scratch_shapes=[pltpu.SemaphoreType.DMA((2,))],
        compiler_params=SMALL,
    )(fragment, *in_hbm(weights))


def lay(own, partner):
    rows, width = own.shape

    def kernel(own_ref, partner_ref, out_ref):
        xl = lax.axis_index("xl")
        for ref, at in ((own_ref, xl), (partner_ref, 1 - xl)):
            out_ref[pl.ds(pl.multiple_of(at * rows, 16), rows), :] = ref[...]

    return pl.pallas_call(
        kernel,
        out_shape=vmem_like((2 * rows, width)),
        in_specs=[WHOLE] * 2,
        out_specs=WHOLE,
        compiler_params=SMALL,
    )(*in_vmem(own, partner))


def gate(values, after):
    def kernel(*refs):
        del refs

    return pl.pallas_call(
        kernel,
        out_shape=[vmem_like(value.shape) for value in values],
        in_specs=[WHOLE] * len(values) + [ANY] * len(after),
        out_specs=[WHOLE] * len(values),
        input_output_aliases={n: n for n in range(len(values))},
        compiler_params=SMALL,
    )(*in_vmem(*values), *after)


def column_blocks(shape, rows, width):
    for n in range(shape[1] // width):
        place, start = divmod(n * shape[0], rows)
        yield n * width, place, start


def pack(planes, grad, other, after):
    halves, steps, rows, width = planes.shape

    def kernel(planes_ref, grad_ref, other_ref, *refs):
        out_ref, entry_ref = refs[-2:]
        out_ref[:halves] = planes_ref[...]
        entry_ref[...] = planes_ref[lax.axis_index("core")]
        for column, place, start in column_blocks(grad.shape, rows, width):
            columns = pl.ds(column, width)
            total = grad_ref[:, columns].astype(jnp.float32) + other_ref[:, columns].astype(jnp.float32)
            out_ref[halves, place, pl.ds(start, grad.shape[0]), :] = total.astype(grad.dtype)

    return pl.pallas_call(
        kernel,
        out_shape=[
            jax.ShapeDtypeStruct((halves + 1, *planes.shape[1:]), planes.dtype),
            vmem_like(planes.shape[1:]),
        ],
        in_specs=[WHOLE] * 3 + [ANY] * len(after),
        out_specs=[WHOLE] * 2,
        compiler_params=pltpu.CompilerParams(vmem_limit_bytes=4 << 20),
    )(*in_vmem(planes, grad, other), *after)


def unpack(mine, theirs, shape):
    behind = mine.shape[0] - 1
    rows, width = mine.shape[2:]

    def kernel(mine_ref, theirs_ref, out_ref):
        for column, place, start in column_blocks(shape, rows, width):
            block = (0, place, pl.ds(start, shape[0]), slice(None))
            total = mine_ref[block].astype(jnp.float32) + theirs_ref[block].astype(jnp.float32)
            out_ref[:, pl.ds(column, width)] = total.astype(out_ref.dtype)

    spec = pl.BlockSpec((1, *mine.shape[1:]), lambda n: (behind, 0, 0, 0))
    return pl.pallas_call(
        kernel,
        grid=(1,),
        out_shape=vmem_like(shape),
        in_specs=[spec] * 2,
        out_specs=WHOLE,
        compiler_params=pltpu.CompilerParams(vmem_limit_bytes=4 << 20),
    )(mine, theirs)


def multiply(blocks, here, mine, theirs, far):
    tokens, depth = blocks[0].shape
    halves, steps, rows, width = here.shape

    def kernel(*refs):
        token_refs, (here_ref, mine_ref, theirs_ref, far_ref) = refs[:CHIPS], refs[CHIPS : CHIPS + 4]
        out_refs, total = refs[CHIPS + 4 : -1], refs[-1]
        zl, core = lax.axis_index("zl"), lax.axis_index("core")
        step = pl.program_id(0)
        sets = ((here_ref, 0), (mine_ref, 3 - 2 * core), (theirs_ref, 1 + 2 * core), (far_ref, 2))
        for n, token_ref in enumerate(token_refs):
            part = None
            for ref, place in sets:
                weight = jnp.concatenate([ref[half, 0] for half in range(halves)], axis=1)
                plane = lax.rem(zl + place, PARTS)
                if n == 0:
                    plane += step * PARTS
                start = pl.multiple_of(plane * rows, 128)
                term = jnp.dot(
                    token_ref[:, pl.ds(start, rows)], weight, preferred_element_type=jnp.float32
                )
                part = term if part is None else part + term
            total[n] = jnp.where(step == 0, part, total[n] + part)

        @pl.when(step == steps - 1)
        def _():
            for n, out_ref in enumerate(out_refs):
                out_ref[...] = total[n].astype(out_ref.dtype)

    weight_spec = pl.BlockSpec((halves, 1, rows, width), lambda s: (0, s, 0, 0))
    token_spec = pl.BlockSpec((tokens, depth // steps), lambda s: (0, s))
    shape = (tokens, halves * width)
    return pl.pallas_call(
        kernel,
        grid=(steps,),
        out_shape=(vmem_like(shape),) * CHIPS,
        in_specs=[WHOLE] + [token_spec] * (CHIPS - 1) + [weight_spec] * 4,
        out_specs=(WHOLE,) * CHIPS,
        scratch_shapes=[pltpu.VMEM((CHIPS, *shape), jnp.float32)],
        compiler_params=pltpu.CompilerParams(vmem_limit_bytes=32 << 20),
        cost_estimate=pl.CostEstimate(
            flops=2 * CHIPS * tokens * depth * halves * width,
            bytes_accessed=2 * (CHIPS * tokens + halves * width) * depth,
            transcendentals=0,
        ),
    )(*in_vmem(blocks[0]), *blocks[1:], here, mine, theirs, far)


def assemble(results, after):
    tokens, width = results[0].shape

    def kernel(*refs):
        out_ref = refs[-1]
        first = quarter(lax.axis_index("xl"))
        for n, ref in enumerate(refs[:CHIPS]):
            start = pl.multiple_of(lax.rem(first + n, CHIPS) * width, 128)
            out_ref[:, pl.ds(start, width)] = ref[...]

    return pl.pallas_call(
        kernel,
        out_shape=jax.ShapeDtypeStruct((tokens, CHIPS * width), results[0].dtype),
        in_specs=[WHOLE] * CHIPS + [ANY],
        out_specs=WHOLE,
        compiler_params=pltpu.CompilerParams(vmem_limit_bytes=4 << 20),
    )(*in_vmem(*results), after)


def from_beside(at):
    return along_z(1 - 2 * at["core"])(at)


def rounded_sum(a, b):
    return (a.astype(jnp.float32) + b.astype(jnp.float32)).astype(a.dtype)


def exchange(weights, tokens, grad, fragment):
    own, give = pick(weights, fragment)
    partner = permute(give, flip("xl"))
    (sent,) = gate((tokens,), (partner,))
    after, across, before = (permute(sent, in_group(step)) for step in (1, 2, 3))
    gathered = lax.all_gather(lay(own, partner), "zh", axis=0, tiled=False)
    here = lax.all_gather(gathered, "core", axis=0, tiled=False)
    other = permute(grad, flip("xh"))
    mine, far = pack(permute(here, from_beside), grad, other, (after, across, before))
    far = permute(far, from_beside)
    theirs = permute(mine, flip("core"))
    far = lax.all_gather(far, "core", axis=0, tiled=False)
    total = unpack(mine, theirs, grad.shape)
    other = permute(total, flip("y"))
    outs = multiply((tokens, after, across, before), here, mine, theirs, far)
    total, other = gate((total, other), outs[1:])
    total = rounded_sum(total, other)
    results = [outs[0]] + [permute(outs[step], in_group(-step)) for step in (1, 2, 3)]
    total = rounded_sum(total, permute(total, flip("y", 2)))
    return results, total


def per_device(weights, momentum, pseudo_grad, tokens, fragment):
    results, total = exchange(weights, tokens, pseudo_grad[0], fragment)
    synced = lax.dynamic_index_in_dim(weights, fragment[0], 0, keepdims=False)
    replicas = lax.axis_size(REP)
    own_grad = pseudo_grad[0].astype(jnp.float32)
    averaged = total.astype(jnp.float32) / replicas
    velocity = MU * momentum.astype(jnp.float32) + averaged
    synced_wide = synced.astype(jnp.float32)
    outer_weights = synced_wide - OUTER_LR * (averaged + MU * velocity)
    inner_weights = synced_wide - own_grad
    blended = (MIX * inner_weights + (1.0 - MIX) * outer_weights).astype(jnp.bfloat16)
    new_momentum = velocity.astype(jnp.bfloat16)
    return (blended[None], new_momentum, assemble(results, new_momentum))


def solution(mesh):
    split = Mesh(mesh.devices.reshape(tuple(SIZES.values())), AXES)
    in_specs = (
        P(None, FSDP, None),
        P(FSDP, None),
        P(REP, FSDP, None),
        P(REP + FSDP, None),
        P(),
    )
    out_specs = (P(REP, FSDP, None), P(FSDP, None), P(REP + FSDP, None))
    return jax.shard_map(
        per_device, mesh=split, in_specs=in_specs, out_specs=out_specs, check_vma=False
    )
```

time: 132 us -> 108 us (0.82)
  starting transfers between devices: 55.9 us -> 41.4 us
  Pallas kernels: 12 us -> 6.09 us
  blocking collectives: 29.1 us -> 34.6 us
  local copies, waits for them, and re-layouts: 5.4 us -> 0.93 us
  waiting for transfers between devices: 24.2 us -> 21.2 us
    ppermute x17 -> x13, starting transfers between devices: 55.9 us -> 41.4 us  [permute(): return lax.ppermute(value, AXES, pairs)]
    all_gather x1 -> x3, blocking collectives: 29.1 us -> 34.6 us  [the longest x1 29.9 us: exchange(): gathered = lax.all_gather(lay(own, partner), 'zh', axis=0, tiled=False)]
    pallas_call x2 -> x7, Pallas kernels: 10.4 us -> 5.35 us  [the longest x1 3.61 us: multiply(): pl.pallas_call(kernel, grid=(steps,), out_shape=(vmem_like(shape),) * CHI...]
    ppermute x17 -> x13, waiting for transfers between devices: 24.2 us -> 21.2 us  [permute(): return lax.ppermute(value, AXES, pairs)]
    slice x2 -> x0, local copies, waits for them, and re-layouts: 1.93 us -> none  [the longest x1 0.99 us: layer_product(): far_low = permute(before[:half], along_z(1))]
    unnamed x24 -> x13, local copies, waits for them, and re-layouts: 2.4 us -> 0.93 us
  transfers between devices with their start and end apart: 17 -> 13, of which waited for: 6 -> 6; matrix products, arithmetic and copies ran while one was open for 5% -> 2% of each run, Pallas kernels for 4% -> 3%
where the time goes in v2:
time: 108 us; the launch traced here: 107 us
  starting transfers between devices  41.4 us (38%)
  blocking collectives  34.6 us (32%)
  waiting for transfers between devices  21.2 us (20%)
  Pallas kernels  6.09 us (6%)
  other arithmetic  2.34 us (2%)
    ppermute x13, starting transfers between devices, permute(): return lax.ppermute(value, AXES, pairs)  41.4 us
    all_gather x1, blocking collectives, exchange(): gathered = lax.all_gather(lay(own, partner), 'zh', axis=0, tiled=False)  29.9 us
    ppermute x13, waiting for transfers between devices, permute(): return lax.ppermute(value, AXES, pairs)  21.2 us
    pallas_call x1, Pallas kernels, multiply(): pl.pallas_call(kernel, grid=(steps,), out_shape=(vmem_like(shape),) * CHI...  3.61 us
    all_gather x1, blocking collectives, exchange(): here = lax.all_gather(gathered, 'core', axis=0, tiled=False)  2.36 us
    all_gather x1, blocking collectives, exchange(): far = lax.all_gather(far, 'core', axis=0, tiled=False)  2.36 us
    convert_element_type x1, other arithmetic, per_device(): new_momentum = velocity.astype(jnp.bfloat16)  2.21 us
  transfers between devices with their start and end apart: 13, of which 6 were waited for; matrix products, arithmetic and copies ran while one was open for 2% of the time, Pallas kernels for 3%

profile of v2, /device:TPU:4, one launch (start us, length us, event | category | flops | bytes accessed | tf_op | source)
XLA Modules:
  0.0 107.5 jit_solution(9336698583681773366)
XLA Ops:
  1.4 1.4 %shard_map.76 = (bf16[192,128]{1,0:T(8,128)(2,1)S(1)}, bf16[192,128]{1,0:T(8,128)(2,1)S(1)}) custom-call(s32[6]{0:T(128)S(1)} %copy-done.3, bf16[6,192,1024]{2,1,0:T(8,128)(2,1)} %weights_ref.1), custom_call_target="tpu_custom_call" | custom-call | tf_op jit(solution)/shard_map/pallas_call | solution.py:106
  2.8 3.1 %collective-permute-start = (bf16[192,128]{1,0:T(8,128)(2,1)S(1)}, bf16[192,128]{1,0:T(8,128)(2,1)S(1)}, u32[]{:S(2)}, u32[]{:S(2)}) collective-permute-start(bf16[192,128]{1,0:T(8,128)(2,1)S(1)} %get-tuple-element.14), channel_id=1, source_target_pairs={{0,1},{1,0},{2,3},{3,2},{4,5},{5,4},{6,7},{7,6},{8,9},{9,8},{10,11... | collective-permute-start | bytes 147464 | tf_op jit(solution)/shard_map/ppermute | solution.py:53
  6.1 2.7 %collective-permute-done.partner_ref.refs_1_ = bf16[192,128]{1,0:T(8,128)(2,1)S(1)} collective-permute-done((bf16[192,128]{1,0:T(8,128)(2,1)S(1)}, bf16[192,128]{1,0:T(8,128)(2,1)S(1)}, u32[]{:S(2)}, u32[]{:S(2)}) %collective-permute-start) | collective-permute-done | bytes 49184 | tf_op jit(solution)/shard_map/ppermute | solution.py:53
  8.8 5.0 %collective-permute-start.5 = (bf16[128,6144]{1,0:T(8,128)(2,1)S(1)}, bf16[128,6144]{1,0:T(8,128)(2,1)S(1)}, u32[]{:S(2)}, u32[]{:S(2)}) collective-permute-start(bf16[128,6144]{1,0:T(8,128)(2,1)S(1)} %shard_map.78), channel_id=1, source_target_pairs={{0,192},{1,193},{2,194},{3,195},{4,196},{5,197},{6,198},{7,199},{8... | collective-permute-start | bytes 4718600 | tf_op jit(solution)/shard_map/ppermute | solution.py:53
  13.9 2.5 %collective-permute-start.4 = (bf16[128,6144]{1,0:T(8,128)(2,1)S(1)}, bf16[128,6144]{1,0:T(8,128)(2,1)S(1)}, u32[]{:S(2)}, u32[]{:S(2)}) collective-permute-start(bf16[128,6144]{1,0:T(8,128)(2,1)S(1)} %shard_map.78), channel_id=1, source_target_pairs={{0,128},{1,129},{2,130},{3,131},{4,132},{5,133},{6,134},{7,135},{8... | collective-permute-start | bytes 4718600 | tf_op jit(solution)/shard_map/ppermute | solution.py:53
  16.4 2.9 %collective-permute-start.3 = (bf16[128,6144]{1,0:T(8,128)(2,1)S(1)}, bf16[128,6144]{1,0:T(8,128)(2,1)S(1)}, u32[]{:S(2)}, u32[]{:S(2)}) collective-permute-start(bf16[128,6144]{1,0:T(8,128)(2,1)S(1)} %shard_map.78), channel_id=1, source_target_pairs={{0,64},{1,65},{2,66},{3,67},{4,68},{5,69},{6,70},{7,71},{8,72},{9,... | collective-permute-start | bytes 4718600 | tf_op jit(solution)/shard_map/ppermute | solution.py:53
  19.3 29.9 %all-gather = bf16[1536,128]{1,0:T(8,128)(2,1)S(1)} all-gather(bf16[384,128]{1,0:T(8,128)(2,1)S(1)} %shard_map.77), channel_id=2, replica_groups=mesh['xh'=2,'y'=4,'core'=2,'zh'=4,'zl'=4,'xl'=2] {'zh'}, dimensions={0}, use_global_device_ids=true | all-gather | bytes 491520 | tf_op jit(solution)/shard_map/all_gather | solution.py:278
  49.2 2.4 %all-gather.1 = bf16[8,384,128]{2,1,0:T(8,128)(2,1)S(1)} all-gather(bf16[4,384,128]{2,1,0:T(8,128)(2,1)S(1)} %bitcast.22), channel_id=3, replica_groups=mesh['xh'=2,'y'=4,'core'=2,'zh'=4,'zl'=4,'xl'=2] {'core'}, dimensions={0}, use_global_device_ids=true | all-gather | bytes 1179648 | tf_op jit(solution)/shard_map/all_gather | solution.py:279
  51.5 3.1 %collective-permute-start.1 = (bf16[2,4,384,128]{3,2,1,0:T(8,128)(2,1)S(1)}, bf16[2,4,384,128]{3,2,1,0:T(8,128)(2,1)S(1)}, u32[]{:S(2)}, u32[]{:S(2)}) collective-permute-start(bf16[2,4,384,128]{3,2,1,0:T(8,128)(2,1)S(1)} %bitcast.14), channel_id=1, source_target_pairs={{0,2},{1,3},{2,4},{3,5},{4,6},{5,7},{6,8},{7,9},{8,10},{9,11},{10,... | collective-permute-start | bytes 2359304 | tf_op jit(solution)/shard_map/ppermute | solution.py:53
  54.7 2.4 %collective-permute-start.2 = (bf16[192,1024]{1,0:T(8,128)(2,1)S(1)}, bf16[192,1024]{1,0:T(8,128)(2,1)S(1)}, u32[]{:S(2)}, u32[]{:S(2)}) collective-permute-start(bf16[192,1024]{1,0:T(8,128)(2,1)S(1)} %bitcast.17), channel_id=1, source_target_pairs={{0,256},{1,257},{2,258},{3,259},{4,260},{5,261},{6,262},{7,263},{8... | collective-permute-start | bytes 1179656 | tf_op jit(solution)/shard_map/ppermute | solution.py:53
  57.1 11.0 %collective-permute-done.2.other_ref = bf16[192,1024]{1,0:T(8,128)(2,1)S(1)} collective-permute-done((bf16[192,1024]{1,0:T(8,128)(2,1)S(1)}, bf16[192,1024]{1,0:T(8,128)(2,1)S(1)}, u32[]{:S(2)}, u32[]{:S(2)}) %collective-permute-start.2) | collective-permute-done | bytes 393248 | tf_op jit(solution)/shard_map/ppermute | solution.py:53
  68.3 1.9 %collective-permute-start.6 = (bf16[3,4,384,128]{3,2,1,0:T(8,128)(2,1)S(1)}, bf16[3,4,384,128]{3,2,1,0:T(8,128)(2,1)S(1)}, u32[]{:S(2)}, u32[]{:S(2)}) collective-permute-start(bf16[3,4,384,128]{3,2,1,0:T(8,128)(2,1)S(1)} %get-tuple-element.15.mine_ref.refs_5_), channel_id=1, source_target_pairs={{0,32},{1,33},{2,34},{3,35},{4,36},{5,37},{6,38},{7,39},{8,40},{9,... | collective-permute-start | bytes 3538952 | tf_op jit(solution)/shard_map/ppermute | solution.py:53
  70.2 3.6 %collective-permute-start.8 = (bf16[4,384,128]{2,1,0:T(8,128)(2,1)S(1)}, bf16[4,384,128]{2,1,0:T(8,128)(2,1)S(1)}, u32[]{:S(2)}, u32[]{:S(2)}) collective-permute-start(bf16[4,384,128]{2,1,0:T(8,128)(2,1)S(1)} %get-tuple-element.16), channel_id=1, source_target_pairs={{0,2},{1,3},{2,4},{3,5},{4,6},{5,7},{6,8},{7,9},{8,10},{9,11},{10,... | collective-permute-start | bytes 1179656 | tf_op jit(solution)/shard_map/ppermute | solution.py:53
  74.0 3.6 %collective-permute-start.7 = (bf16[192,1024]{1,0:T(8,128)(2,1)S(1)}, bf16[192,1024]{1,0:T(8,128)(2,1)S(1)}, u32[]{:S(2)}, u32[]{:S(2)}) collective-permute-start(bf16[192,1024]{1,0:T(8,128)(2,1)S(1)} %shard_map.80.refs_0_), channel_id=1, source_target_pairs={{0,64},{1,65},{2,66},{3,67},{4,68},{5,69},{6,70},{7,71},{8,72},{9,... | collective-permute-start | bytes 1179656 | tf_op jit(solution)/shard_map/ppermute | solution.py:53
  77.5 3.6 %collective-permute-done.8 = bf16[4,384,128]{2,1,0:T(8,128)(2,1)S(1)} collective-permute-done((bf16[4,384,128]{2,1,0:T(8,128)(2,1)S(1)}, bf16[4,384,128]{2,1,0:T(8,128)(2,1)S(1)}, u32[]{:S(2)}, u32[]{:S(2)}) %collective-permute-start.8) | collective-permute-done | bytes 393248 | tf_op jit(solution)/shard_map/ppermute | solution.py:53
  81.1 2.4 %all-gather.2 = bf16[8,384,128]{2,1,0:T(8,128)(2,1)S(1)} all-gather(bf16[4,384,128]{2,1,0:T(8,128)(2,1)S(1)} %collective-permute-done.8), channel_id=4, replica_groups=mesh['xh'=2,'y'=4,'core'=2,'zh'=4,'zl'=4,'xl'=2] {'core'}, dimensions={0}, use_global_device_ids=true | all-gather | bytes 1179648 | tf_op jit(solution)/shard_map/all_gather | solution.py:284
  83.5 3.6 %shard_map.81 = (bf16[128,256]{1,0:T(8,128)(2,1)S(1)}, bf16[128,256]{1,0:T(8,128)(2,1)S(1)}, bf16[128,256]{1,0:T(8,128)(2,1)S(1)}, bf16[128,256]{1,0:T(8,128)(2,1)S(1)}) custom-call(bf16[128,6144]{1,0:T(8,128)(2,1)S(1)} %copy-done, bf16[128,6144]{1,0:T(8,128)(2,1)S(1)} %collective-permute-done.3.refs_0_.refs_1_, ...), custom_call_target="tpu_custom_call" | custom-call | flops 1610612736 | bytes 9437184 | tf_op jit(solution)/shard_map/pallas_call | solution.py:230
  87.9 3.3 %collective-permute-start.9 = (bf16[192,1024]{1,0:T(8,128)(2,1)S(1)}, bf16[192,1024]{1,0:T(8,128)(2,1)S(1)}, u32[]{:S(2)}, u32[]{:S(2)}) collective-permute-start(bf16[192,1024]{1,0:T(8,128)(2,1)S(1)} %add_convert_fusion.1), channel_id=1, source_target_pairs={{0,128},{1,129},{2,130},{3,131},{4,132},{5,133},{6,134},{7,135},{8... | collective-permute-start | bytes 1179656 | tf_op jit(solution)/shard_map/ppermute | solution.py:53
  91.4 4.7 %collective-permute-start.10 = (bf16[128,256]{1,0:T(8,128)(2,1)S(1)}, bf16[128,256]{1,0:T(8,128)(2,1)S(1)}, u32[]{:S(2)}, u32[]{:S(2)}) collective-permute-start(bf16[128,256]{1,0:T(8,128)(2,1)S(1)} %get-tuple-element.17.refs_2_), channel_id=1, source_target_pairs={{0,192},{1,193},{2,194},{3,195},{4,196},{5,197},{6,198},{7,199},{8... | collective-permute-start | bytes 196616 | tf_op jit(solution)/shard_map/ppermute | solution.py:53
  96.1 3.2 %collective-permute-start.11 = (bf16[128,256]{1,0:T(8,128)(2,1)S(1)}, bf16[128,256]{1,0:T(8,128)(2,1)S(1)}, u32[]{:S(2)}, u32[]{:S(2)}) collective-permute-start(bf16[128,256]{1,0:T(8,128)(2,1)S(1)} %get-tuple-element.18.refs_3_), channel_id=1, source_target_pairs={{0,128},{1,129},{2,130},{3,131},{4,132},{5,133},{6,134},{7,135},{8... | collective-permute-start | bytes 196616 | tf_op jit(solution)/shard_map/ppermute | solution.py:53
  99.3 1.9 %collective-permute-start.12 = (bf16[128,256]{1,0:T(8,128)(2,1)S(1)}, bf16[128,256]{1,0:T(8,128)(2,1)S(1)}, u32[]{:S(2)}, u32[]{:S(2)}) collective-permute-start(bf16[128,256]{1,0:T(8,128)(2,1)S(1)} %get-tuple-element.19.refs_4_), channel_id=1, source_target_pairs={{0,64},{1,65},{2,66},{3,67},{4,68},{5,69},{6,70},{7,71},{8,72},{9,... | collective-permute-start | bytes 196616 | tf_op jit(solution)/shard_map/ppermute | solution.py:53
  101.3 1.2 %collective-permute-done.9 = bf16[192,1024]{1,0:T(8,128)(2,1)S(1)} collective-permute-done((bf16[192,1024]{1,0:T(8,128)(2,1)S(1)}, bf16[192,1024]{1,0:T(8,128)(2,1)S(1)}, u32[]{:S(2)}, u32[]{:S(2)}) %collective-permute-start.9) | collective-permute-done | bytes 393248 | tf_op jit(solution)/shard_map/ppermute | solution.py:53
  102.5 2.2 %fusion.3 = (bf16[192,1024]{1,0:T(8,128)(2,1)S(1)}, bf16[1,192,1024]{2,1,0:T(8,128)(2,1)}) fusion(bf16[192,1024]{1,0:T(8,128)(2,1)S(1)} %copy-done.5, bf16[192,1024]{1,0:T(8,128)(2,1)S(1)} %collective-permute-done.9, bf16[192,1024]{1,0:T(8,128)(2,1)S(1)} %add_convert_fusion.1, bf16[1,192,1024]{2,1,0:T(8,128)(2,1)S(1)} %copy-done.1, ...), kind=kLoop, calls=%fused_computation.6 | loop fusion | flops 3932160 | bytes 2752516 | tf_op jit(solution)/shard_map/convert_element_type | solution.py:306
  104.7 2.0 %collective-permute-done.12.refs_3_ = bf16[128,256]{1,0:T(8,128)(2,1)S(1)} collective-permute-done((bf16[128,256]{1,0:T(8,128)(2,1)S(1)}, bf16[128,256]{1,0:T(8,128)(2,1)S(1)}, u32[]{:S(2)}, u32[]{:S(2)}) %collective-permute-start.12) | collective-permute-done | bytes 65568 | tf_op jit(solution)/shard_map/ppermute | solution.py:53
  (28 shorter events, 2.8 us)
Async XLA Ops:
  0.6 5.3 %copy-start = (bf16[128,6144]{1,0:T(8,128)(2,1)S(1)}, bf16[128,6144]{1,0:T(8,128)(2,1)}, u32[]{:S(2)}) copy-start(bf16[128,6144]{1,0:T(8,128)(2,1)} %refs_0_.2) | copy-start | bytes 4718596
  0.6 0.8 copy-start.3
  2.8 6.0 %collective-permute-start = (bf16[192,128]{1,0:T(8,128)(2,1)S(1)}, bf16[192,128]{1,0:T(8,128)(2,1)S(1)}, u32[]{:S(2)}, u32[]{:S(2)}) collective-permute-start(bf16[192,128]{1,0:T(8,128)(2,1)S(1)} %get-tuple-element.14), channel_id=1, source_target_pairs={{0,1},{1,0},{2,3},{3,2},{4,5},{5,4},{6,7},{7,6},{8,9},{9,8},{10,11... | collective-permute-start | bytes 147464 | tf_op jit(solution)/shard_map/ppermute | solution.py:53
  8.8 45.9 %copy-start.1 = (bf16[1,192,1024]{2,1,0:T(8,128)(2,1)S(1)}, bf16[1,192,1024]{2,1,0:T(8,128)(2,1)}, u32[]{:S(2)}) copy-start(bf16[1,192,1024]{2,1,0:T(8,128)(2,1)} %param.7) | copy-start | bytes 1179652
  8.8 59.3 %collective-permute-start.5 = (bf16[128,6144]{1,0:T(8,128)(2,1)S(1)}, bf16[128,6144]{1,0:T(8,128)(2,1)S(1)}, u32[]{:S(2)}, u32[]{:S(2)}) collective-permute-start(bf16[128,6144]{1,0:T(8,128)(2,1)S(1)} %shard_map.78), channel_id=1, source_target_pairs={{0,192},{1,193},{2,194},{3,195},{4,196},{5,197},{6,198},{7,199},{8... | collective-permute-start | bytes 4718600 | tf_op jit(solution)/shard_map/ppermute | solution.py:53
  13.9 54.2 %collective-permute-start.4 = (bf16[128,6144]{1,0:T(8,128)(2,1)S(1)}, bf16[128,6144]{1,0:T(8,128)(2,1)S(1)}, u32[]{:S(2)}, u32[]{:S(2)}) collective-permute-start(bf16[128,6144]{1,0:T(8,128)(2,1)S(1)} %shard_map.78), channel_id=1, source_target_pairs={{0,128},{1,129},{2,130},{3,131},{4,132},{5,133},{6,134},{7,135},{8... | collective-permute-start | bytes 4718600 | tf_op jit(solution)/shard_map/ppermute | solution.py:53
  16.4 51.7 %collective-permute-start.3 = (bf16[128,6144]{1,0:T(8,128)(2,1)S(1)}, bf16[128,6144]{1,0:T(8,128)(2,1)S(1)}, u32[]{:S(2)}, u32[]{:S(2)}) collective-permute-start(bf16[128,6144]{1,0:T(8,128)(2,1)S(1)} %shard_map.78), channel_id=1, source_target_pairs={{0,64},{1,65},{2,66},{3,67},{4,68},{5,69},{6,70},{7,71},{8,72},{9,... | collective-permute-start | bytes 4718600 | tf_op jit(solution)/shard_map/ppermute | solution.py:53
  51.5 16.6 %collective-permute-start.1 = (bf16[2,4,384,128]{3,2,1,0:T(8,128)(2,1)S(1)}, bf16[2,4,384,128]{3,2,1,0:T(8,128)(2,1)S(1)}, u32[]{:S(2)}, u32[]{:S(2)}) collective-permute-start(bf16[2,4,384,128]{3,2,1,0:T(8,128)(2,1)S(1)} %bitcast.14), channel_id=1, source_target_pairs={{0,2},{1,3},{2,4},{3,5},{4,6},{5,7},{6,8},{7,9},{8,10},{9,11},{10,... | collective-permute-start | bytes 2359304 | tf_op jit(solution)/shard_map/ppermute | solution.py:53
  54.7 13.4 %collective-permute-start.2 = (bf16[192,1024]{1,0:T(8,128)(2,1)S(1)}, bf16[192,1024]{1,0:T(8,128)(2,1)S(1)}, u32[]{:S(2)}, u32[]{:S(2)}) collective-permute-start(bf16[192,1024]{1,0:T(8,128)(2,1)S(1)} %bitcast.17), channel_id=1, source_target_pairs={{0,256},{1,257},{2,258},{3,259},{4,260},{5,261},{6,262},{7,263},{8... | collective-permute-start | bytes 1179656 | tf_op jit(solution)/shard_map/ppermute | solution.py:53
  68.3 5.5 %collective-permute-start.6 = (bf16[3,4,384,128]{3,2,1,0:T(8,128)(2,1)S(1)}, bf16[3,4,384,128]{3,2,1,0:T(8,128)(2,1)S(1)}, u32[]{:S(2)}, u32[]{:S(2)}) collective-permute-start(bf16[3,4,384,128]{3,2,1,0:T(8,128)(2,1)S(1)} %get-tuple-element.15.mine_ref.refs_5_), channel_id=1, source_target_pairs={{0,32},{1,33},{2,34},{3,35},{4,36},{5,37},{6,38},{7,39},{8,40},{9,... | collective-permute-start | bytes 3538952 | tf_op jit(solution)/shard_map/ppermute | solution.py:53
  70.2 10.9 %collective-permute-start.8 = (bf16[4,384,128]{2,1,0:T(8,128)(2,1)S(1)}, bf16[4,384,128]{2,1,0:T(8,128)(2,1)S(1)}, u32[]{:S(2)}, u32[]{:S(2)}) collective-permute-start(bf16[4,384,128]{2,1,0:T(8,128)(2,1)S(1)} %get-tuple-element.16), channel_id=1, source_target_pairs={{0,2},{1,3},{2,4},{3,5},{4,6},{5,7},{6,8},{7,9},{8,10},{9,11},{10,... | collective-permute-start | bytes 1179656 | tf_op jit(solution)/shard_map/ppermute | solution.py:53
  74.0 13.8 %collective-permute-start.7 = (bf16[192,1024]{1,0:T(8,128)(2,1)S(1)}, bf16[192,1024]{1,0:T(8,128)(2,1)S(1)}, u32[]{:S(2)}, u32[]{:S(2)}) collective-permute-start(bf16[192,1024]{1,0:T(8,128)(2,1)S(1)} %shard_map.80.refs_0_), channel_id=1, source_target_pairs={{0,64},{1,65},{2,66},{3,67},{4,68},{5,69},{6,70},{7,71},{8,72},{9,... | collective-permute-start | bytes 1179656 | tf_op jit(solution)/shard_map/ppermute | solution.py:53
  87.1 4.2 %copy-start.4 = (s32[6]{0:T(128)S(1)}, s32[6]{0:T(128)}, u32[]{:S(2)}) copy-start(s32[6]{0:T(128)} %fragment_ref.1) | copy-start | bytes 76
  87.1 15.4 %copy-start.5 = (bf16[192,1024]{1,0:T(8,128)(2,1)S(1)}, bf16[192,1024]{1,0:T(8,128)(2,1)}, u32[]{:S(2)}) copy-start(bf16[192,1024]{1,0:T(8,128)(2,1)} %param.6) | copy-start | bytes 1179652
  87.9 14.5 %collective-permute-start.9 = (bf16[192,1024]{1,0:T(8,128)(2,1)S(1)}, bf16[192,1024]{1,0:T(8,128)(2,1)S(1)}, u32[]{:S(2)}, u32[]{:S(2)}) collective-permute-start(bf16[192,1024]{1,0:T(8,128)(2,1)S(1)} %add_convert_fusion.1), channel_id=1, source_target_pairs={{0,128},{1,129},{2,130},{3,131},{4,132},{5,133},{6,134},{7,135},{8... | collective-permute-start | bytes 1179656 | tf_op jit(solution)/shard_map/ppermute | solution.py:53
  91.4 13.3 %collective-permute-start.10 = (bf16[128,256]{1,0:T(8,128)(2,1)S(1)}, bf16[128,256]{1,0:T(8,128)(2,1)S(1)}, u32[]{:S(2)}, u32[]{:S(2)}) collective-permute-start(bf16[128,256]{1,0:T(8,128)(2,1)S(1)} %get-tuple-element.17.refs_2_), channel_id=1, source_target_pairs={{0,192},{1,193},{2,194},{3,195},{4,196},{5,197},{6,198},{7,199},{8... | collective-permute-start | bytes 196616 | tf_op jit(solution)/shard_map/ppermute | solution.py:53
  96.1 8.6 %collective-permute-start.11 = (bf16[128,256]{1,0:T(8,128)(2,1)S(1)}, bf16[128,256]{1,0:T(8,128)(2,1)S(1)}, u32[]{:S(2)}, u32[]{:S(2)}) collective-permute-start(bf16[128,256]{1,0:T(8,128)(2,1)S(1)} %get-tuple-element.18.refs_3_), channel_id=1, source_target_pairs={{0,128},{1,129},{2,130},{3,131},{4,132},{5,133},{6,134},{7,135},{8... | collective-permute-start | bytes 196616 | tf_op jit(solution)/shard_map/ppermute | solution.py:53
  99.3 7.4 %collective-permute-start.12 = (bf16[128,256]{1,0:T(8,128)(2,1)S(1)}, bf16[128,256]{1,0:T(8,128)(2,1)S(1)}, u32[]{:S(2)}, u32[]{:S(2)}) collective-permute-start(bf16[128,256]{1,0:T(8,128)(2,1)S(1)} %get-tuple-element.19.refs_4_), channel_id=1, source_target_pairs={{0,64},{1,65},{2,66},{3,67},{4,68},{5,69},{6,70},{7,71},{8,72},{9,... | collective-permute-start | bytes 196616 | tf_op jit(solution)/shard_map/ppermute | solution.py:53
  104.7 2.8 %copy-start.2 = (bf16[192,1024]{1,0:T(8,128)(2,1)}, bf16[192,1024]{1,0:T(8,128)(2,1)S(1)}, u32[]{:S(2)}) copy-start(bf16[192,1024]{1,0:T(8,128)(2,1)S(1)} %get-tuple-element.23.refs_4_) | copy-start | bytes 1179652

commit v3 on v2

--- a/solution.py
+++ b/solution.py
@@ -144,55 +144,17 @@
     )(*in_vmem(*values), *after)
 
 
-def column_blocks(shape, rows, width):
-    for n in range(shape[1] // width):
-        place, start = divmod(n * shape[0], rows)
-        yield n * width, place, start
-
-
-def pack(planes, grad, other, after):
-    halves, steps, rows, width = planes.shape
-
-    def kernel(planes_ref, grad_ref, other_ref, *refs):
-        out_ref, entry_ref = refs[-2:]
-        out_ref[:halves] = planes_ref[...]
-        entry_ref[...] = planes_ref[lax.axis_index("core")]
-        for column, place, start in column_blocks(grad.shape, rows, width):
-            columns = pl.ds(column, width)
-            total = grad_ref[:, columns].astype(jnp.float32) + other_ref[:, columns].astype(jnp.float32)
-            out_ref[halves, place, pl.ds(start, grad.shape[0]), :] = total.astype(grad.dtype)
-
-    return pl.pallas_call(
-        kernel,
-        out_shape=[
-            jax.ShapeDtypeStruct((halves + 1, *planes.shape[1:]), planes.dtype),
-            vmem_like(planes.shape[1:]),
-        ],
-        in_specs=[WHOLE] * 3 + [ANY] * len(after),
-        out_specs=[WHOLE] * 2,
-        compiler_params=pltpu.CompilerParams(vmem_limit_bytes=4 << 20),
-    )(*in_vmem(planes, grad, other), *after)
-
-
-def unpack(mine, theirs, shape):
-    behind = mine.shape[0] - 1
-    rows, width = mine.shape[2:]
-
-    def kernel(mine_ref, theirs_ref, out_ref):
-        for column, place, start in column_blocks(shape, rows, width):
-            block = (0, place, pl.ds(start, shape[0]), slice(None))
-            total = mine_ref[block].astype(jnp.float32) + theirs_ref[block].astype(jnp.float32)
-            out_ref[:, pl.ds(column, width)] = total.astype(out_ref.dtype)
-
-    spec = pl.BlockSpec((1, *mine.shape[1:]), lambda n: (behind, 0, 0, 0))
-    return pl.pallas_call(
-        kernel,
-        grid=(1,),
-        out_shape=vmem_like(shape),
-        in_specs=[spec] * 2,
+def choose(value, after):
+    def kernel(value_ref, *refs):
+        refs[-1][...] = value_ref[lax.axis_index("core")]
+
+    return pl.pallas_call(
+        kernel,
+        out_shape=vmem_like(value.shape[1:]),
+        in_specs=[WHOLE] + [ANY] * len(after),
         out_specs=WHOLE,
-        compiler_params=pltpu.CompilerParams(vmem_limit_bytes=4 << 20),
-    )(mine, theirs)
+        compiler_params=SMALL,
+    )(*in_vmem(value), *after)
 
 
 def multiply(blocks, here, mine, theirs, far):
@@ -266,6 +228,11 @@
     return along_z(1 - 2 * at["core"])(at)
 
 
+def beside_y(at):
+    at["y"] = (at["y"] + 1 - 2 * at["core"]) % SIZES["y"]
+    return at
+
+
 def rounded_sum(a, b):
     return (a.astype(jnp.float32) + b.astype(jnp.float32)).astype(a.dtype)
 
@@ -275,20 +242,22 @@
     partner = permute(give, flip("xl"))
     (sent,) = gate((tokens,), (partner,))
     after, across, before = (permute(sent, in_group(step)) for step in (1, 2, 3))
+    other = permute(grad, flip("core"))
     gathered = lax.all_gather(lay(own, partner), "zh", axis=0, tiled=False)
     here = lax.all_gather(gathered, "core", axis=0, tiled=False)
-    other = permute(grad, flip("xh"))
-    mine, far = pack(permute(here, from_beside), grad, other, (after, across, before))
-    far = permute(far, from_beside)
+    mine = permute(here, from_beside)
+    total = rounded_sum(grad, other)
+    other = permute(total, flip("y", 2))
+    far = permute(choose(mine, (after, across, before)), from_beside)
     theirs = permute(mine, flip("core"))
     far = lax.all_gather(far, "core", axis=0, tiled=False)
-    total = unpack(mine, theirs, grad.shape)
-    other = permute(total, flip("y"))
+    total = rounded_sum(total, other)
+    other = permute(total, beside_y)
     outs = multiply((tokens, after, across, before), here, mine, theirs, far)
     total, other = gate((total, other), outs[1:])
     total = rounded_sum(total, other)
     results = [outs[0]] + [permute(outs[step], in_group(-step)) for step in (1, 2, 3)]
-    total = rounded_sum(total, permute(total, flip("y", 2)))
+    total = rounded_sum(total, permute(total, flip("xh")))
     return results, total
 
 

time: 108 us -> 106 us (0.981)
  the two profiles are of different devices: /device:TPU:4 before, /device:TPU:2 now
where the time goes in v3:
time: 106 us
  starting transfers between devices  42.8 us (40%)
  blocking collectives  32.7 us (31%)
  waiting for transfers between devices  19.7 us (19%)
  Pallas kernels  5.81 us (5%)
  other arithmetic  2.61 us (2%)
    ppermute x14, starting transfers between devices, permute(): return lax.ppermute(value, AXES, pairs)  42.8 us
    all_gather x1, blocking collectives, exchange(): gathered = lax.all_gather(lay(own, partner), 'zh', axis=0, tiled=False)  28 us
    ppermute x14, waiting for transfers between devices, permute(): return lax.ppermute(value, AXES, pairs)  19.7 us
    pallas_call x1, Pallas kernels, multiply(): pl.pallas_call(kernel, grid=(steps,), out_shape=(vmem_like(shape),) * CHI...  3.6 us
    all_gather x1, blocking collectives, exchange(): here = lax.all_gather(gathered, 'core', axis=0, tiled=False)  2.36 us
    all_gather x1, blocking collectives, exchange(): far = lax.all_gather(far, 'core', axis=0, tiled=False)  2.36 us
    convert_element_type x1, other arithmetic, per_device(): new_momentum = velocity.astype(jnp.bfloat16)  2.21 us
  transfers between devices with their start and end apart: 14, of which 7 were waited for; matrix products, arithmetic and copies ran while one was open for 2% of the time, Pallas kernels for 3%

profile of v3, /device:TPU:2, one launch (start us, length us, event | category | flops | bytes accessed | tf_op | source)
XLA Modules:
  0.0 105.6 jit_solution(8427227865291782080)
XLA Ops:
  2.8 7.8 %collective-permute-start.3 = (bf16[192,128]{1,0:T(8,128)(2,1)S(1)}, bf16[192,128]{1,0:T(8,128)(2,1)S(1)}, u32[]{:S(2)}, u32[]{:S(2)}) collective-permute-start(bf16[192,128]{1,0:T(8,128)(2,1)S(1)} %get-tuple-element.11), channel_id=1, source_target_pairs={{0,1},{1,0},{2,3},{3,2},{4,5},{5,4},{6,7},{7,6},{8,9},{9,8},{10,11... | collective-permute-start | bytes 147464 | tf_op jit(solution)/shard_map/ppermute | solution.py:53
  10.8 2.4 %collective-permute-done.3.refs_1_.partner_ref = bf16[192,128]{1,0:T(8,128)(2,1)S(1)} collective-permute-done((bf16[192,128]{1,0:T(8,128)(2,1)S(1)}, bf16[192,128]{1,0:T(8,128)(2,1)S(1)}, u32[]{:S(2)}, u32[]{:S(2)}) %collective-permute-start.3) | collective-permute-done | bytes 49184 | tf_op jit(solution)/shard_map/ppermute | solution.py:53
  13.2 2.0 %collective-permute-start.4 = (bf16[128,6144]{1,0:T(8,128)(2,1)S(1)}, bf16[128,6144]{1,0:T(8,128)(2,1)S(1)}, u32[]{:S(2)}, u32[]{:S(2)}) collective-permute-start(bf16[128,6144]{1,0:T(8,128)(2,1)S(1)} %shard_map.77), channel_id=1, source_target_pairs={{0,64},{1,65},{2,66},{3,67},{4,68},{5,69},{6,70},{7,71},{8,72},{9,... | collective-permute-start | bytes 4718600 | tf_op jit(solution)/shard_map/ppermute | solution.py:53
  15.3 2.0 %collective-permute-start.5 = (bf16[128,6144]{1,0:T(8,128)(2,1)S(1)}, bf16[128,6144]{1,0:T(8,128)(2,1)S(1)}, u32[]{:S(2)}, u32[]{:S(2)}) collective-permute-start(bf16[128,6144]{1,0:T(8,128)(2,1)S(1)} %shard_map.77), channel_id=1, source_target_pairs={{0,128},{1,129},{2,130},{3,131},{4,132},{5,133},{6,134},{7,135},{8... | collective-permute-start | bytes 4718600 | tf_op jit(solution)/shard_map/ppermute | solution.py:53
  17.2 5.1 %collective-permute-start.6 = (bf16[128,6144]{1,0:T(8,128)(2,1)S(1)}, bf16[128,6144]{1,0:T(8,128)(2,1)S(1)}, u32[]{:S(2)}, u32[]{:S(2)}) collective-permute-start(bf16[128,6144]{1,0:T(8,128)(2,1)S(1)} %shard_map.77), channel_id=1, source_target_pairs={{0,192},{1,193},{2,194},{3,195},{4,196},{5,197},{6,198},{7,199},{8... | collective-permute-start | bytes 4718600 | tf_op jit(solution)/shard_map/ppermute | solution.py:53
  22.4 28.0 %all-gather = bf16[1536,128]{1,0:T(8,128)(2,1)S(1)} all-gather(bf16[384,128]{1,0:T(8,128)(2,1)S(1)} %shard_map.78), channel_id=2, replica_groups=mesh['xh'=2,'y'=4,'core'=2,'zh'=4,'zl'=4,'xl'=2] {'zh'}, dimensions={0}, use_global_device_ids=true | all-gather | bytes 491520 | tf_op jit(solution)/shard_map/all_gather | solution.py:246
  50.4 2.4 %all-gather.1 = bf16[8,384,128]{2,1,0:T(8,128)(2,1)S(1)} all-gather(bf16[4,384,128]{2,1,0:T(8,128)(2,1)S(1)} %bitcast.21), channel_id=3, replica_groups=mesh['xh'=2,'y'=4,'core'=2,'zh'=4,'zl'=4,'xl'=2] {'core'}, dimensions={0}, use_global_device_ids=true | all-gather | bytes 1179648 | tf_op jit(solution)/shard_map/all_gather | solution.py:247
  52.7 3.2 %collective-permute-start.7 = (bf16[2,4,384,128]{3,2,1,0:T(8,128)(2,1)S(1)}, bf16[2,4,384,128]{3,2,1,0:T(8,128)(2,1)S(1)}, u32[]{:S(2)}, u32[]{:S(2)}) collective-permute-start(bf16[2,4,384,128]{3,2,1,0:T(8,128)(2,1)S(1)} %bitcast.15), channel_id=1, source_target_pairs={{0,2},{1,3},{2,4},{3,5},{4,6},{5,7},{6,8},{7,9},{8,10},{9,11},{10,... | collective-permute-start | bytes 2359304 | tf_op jit(solution)/shard_map/ppermute | solution.py:53
  56.0 1.9 %collective-permute-start = (bf16[192,1024]{1,0:T(8,128)(2,1)S(1)}, bf16[192,1024]{1,0:T(8,128)(2,1)S(1)}, u32[]{:S(2)}, u32[]{:S(2)}) collective-permute-start(bf16[192,1024]{1,0:T(8,128)(2,1)S(1)} %bitcast.22), channel_id=1, source_target_pairs={{0,32},{1,33},{2,34},{3,35},{4,36},{5,37},{6,38},{7,39},{8,40},{9,... | collective-permute-start | bytes 1179656 | tf_op jit(solution)/shard_map/ppermute | solution.py:53
  59.7 1.9 %collective-permute-start.1 = (bf16[192,1024]{1,0:T(8,128)(2,1)S(1)}, bf16[192,1024]{1,0:T(8,128)(2,1)S(1)}, u32[]{:S(2)}, u32[]{:S(2)}) collective-permute-start(bf16[192,1024]{1,0:T(8,128)(2,1)S(1)} %fusion), channel_id=1, source_target_pairs={{0,128},{1,129},{2,130},{3,131},{4,132},{5,133},{6,134},{7,135},{8... | collective-permute-start | bytes 1179656 | tf_op jit(solution)/shard_map/ppermute | solution.py:53
  61.7 6.1 %collective-permute-done.7.value_ref.refs_5_ = bf16[2,4,384,128]{3,2,1,0:T(8,128)(2,1)S(1)} collective-permute-done((bf16[2,4,384,128]{3,2,1,0:T(8,128)(2,1)S(1)}, bf16[2,4,384,128]{3,2,1,0:T(8,128)(2,1)S(1)}, u32[]{:S(2)}, u32[]{:S(2)}) %collective-permute-start.7) | collective-permute-done | bytes 786464 | tf_op jit(solution)/shard_map/ppermute | solution.py:53
  67.8 1.9 %collective-permute-start.8 = (bf16[2,4,384,128]{3,2,1,0:T(8,128)(2,1)S(1)}, bf16[2,4,384,128]{3,2,1,0:T(8,128)(2,1)S(1)}, u32[]{:S(2)}, u32[]{:S(2)}) collective-permute-start(bf16[2,4,384,128]{3,2,1,0:T(8,128)(2,1)S(1)} %collective-permute-done.7.value_ref.refs_5_), channel_id=1, source_target_pairs={{0,32},{1,33},{2,34},{3,35},{4,36},{5,37},{6,38},{7,39},{8,40},{9,... | collective-permute-start | bytes 2359304 | tf_op jit(solution)/shard_map/ppermute | solution.py:53
  69.8 2.0 %collective-permute-start.9 = (bf16[4,384,128]{2,1,0:T(8,128)(2,1)S(1)}, bf16[4,384,128]{2,1,0:T(8,128)(2,1)S(1)}, u32[]{:S(2)}, u32[]{:S(2)}) collective-permute-start(bf16[4,384,128]{2,1,0:T(8,128)(2,1)S(1)} %shard_map.79), channel_id=1, source_target_pairs={{0,2},{1,3},{2,4},{3,5},{4,6},{5,7},{6,8},{7,9},{8,10},{9,11},{10,... | collective-permute-start | bytes 1179656 | tf_op jit(solution)/shard_map/ppermute | solution.py:53
  71.9 2.4 %collective-permute-done.1 = bf16[192,1024]{1,0:T(8,128)(2,1)S(1)} collective-permute-done((bf16[192,1024]{1,0:T(8,128)(2,1)S(1)}, bf16[192,1024]{1,0:T(8,128)(2,1)S(1)}, u32[]{:S(2)}, u32[]{:S(2)}) %collective-permute-start.1) | collective-permute-done | bytes 393248 | tf_op jit(solution)/shard_map/ppermute | solution.py:53
  74.4 2.5 %collective-permute-start.2 = (bf16[192,1024]{1,0:T(8,128)(2,1)S(1)}, bf16[192,1024]{1,0:T(8,128)(2,1)S(1)}, u32[]{:S(2)}, u32[]{:S(2)}) collective-permute-start(bf16[192,1024]{1,0:T(8,128)(2,1)S(1)} %add_convert_fusion.2.refs_0_), channel_id=1, source_target_pairs={{0,64},{1,65},{2,66},{3,67},{4,68},{5,69},{6,70},{7,71},{8,72},{9,... | collective-permute-start | bytes 1179656 | tf_op jit(solution)/shard_map/ppermute | solution.py:53
  76.9 3.8 %collective-permute-done.9 = bf16[4,384,128]{2,1,0:T(8,128)(2,1)S(1)} collective-permute-done((bf16[4,384,128]{2,1,0:T(8,128)(2,1)S(1)}, bf16[4,384,128]{2,1,0:T(8,128)(2,1)S(1)}, u32[]{:S(2)}, u32[]{:S(2)}) %collective-permute-start.9) | collective-permute-done | bytes 393248 | tf_op jit(solution)/shard_map/ppermute | solution.py:53
  80.7 2.4 %all-gather.2 = bf16[8,384,128]{2,1,0:T(8,128)(2,1)S(1)} all-gather(bf16[4,384,128]{2,1,0:T(8,128)(2,1)S(1)} %collective-permute-done.9), channel_id=4, replica_groups=mesh['xh'=2,'y'=4,'core'=2,'zh'=4,'zl'=4,'xl'=2] {'core'}, dimensions={0}, use_global_device_ids=true | all-gather | bytes 1179648 | tf_op jit(solution)/shard_map/all_gather | solution.py:253
  83.0 3.6 %shard_map.80 = (bf16[128,256]{1,0:T(8,128)(2,1)S(1)}, bf16[128,256]{1,0:T(8,128)(2,1)S(1)}, bf16[128,256]{1,0:T(8,128)(2,1)S(1)}, bf16[128,256]{1,0:T(8,128)(2,1)S(1)}) custom-call(bf16[128,6144]{1,0:T(8,128)(2,1)S(1)} %copy-done, bf16[128,6144]{1,0:T(8,128)(2,1)S(1)} %collective-permute-done.4.refs_0_.refs_1_, ...), custom_call_target="tpu_custom_call" | custom-call | flops 1610612736 | bytes 9437184 | tf_op jit(solution)/shard_map/pallas_call | solution.py:192
  86.8 2.9 %collective-permute-start.10 = (bf16[192,1024]{1,0:T(8,128)(2,1)S(1)}, bf16[192,1024]{1,0:T(8,128)(2,1)S(1)}, u32[]{:S(2)}, u32[]{:S(2)}) collective-permute-start(bf16[192,1024]{1,0:T(8,128)(2,1)S(1)} %add_convert_fusion.1), channel_id=1, source_target_pairs={{0,256},{1,257},{2,258},{3,259},{4,260},{5,261},{6,262},{7,263},{8... | collective-permute-start | bytes 1179656 | tf_op jit(solution)/shard_map/ppermute | solution.py:53
  89.9 1.9 %collective-permute-start.11 = (bf16[128,256]{1,0:T(8,128)(2,1)S(1)}, bf16[128,256]{1,0:T(8,128)(2,1)S(1)}, u32[]{:S(2)}, u32[]{:S(2)}) collective-permute-start(bf16[128,256]{1,0:T(8,128)(2,1)S(1)} %get-tuple-element.13.refs_2_), channel_id=1, source_target_pairs={{0,192},{1,193},{2,194},{3,195},{4,196},{5,197},{6,198},{7,199},{8... | collective-permute-start | bytes 196616 | tf_op jit(solution)/shard_map/ppermute | solution.py:53
  91.8 5.6 %collective-permute-start.12 = (bf16[128,256]{1,0:T(8,128)(2,1)S(1)}, bf16[128,256]{1,0:T(8,128)(2,1)S(1)}, u32[]{:S(2)}, u32[]{:S(2)}) collective-permute-start(bf16[128,256]{1,0:T(8,128)(2,1)S(1)} %get-tuple-element.14.refs_3_), channel_id=1, source_target_pairs={{0,128},{1,129},{2,130},{3,131},{4,132},{5,133},{6,134},{7,135},{8... | collective-permute-start | bytes 196616 | tf_op jit(solution)/shard_map/ppermute | solution.py:53
  97.4 1.9 %collective-permute-start.13 = (bf16[128,256]{1,0:T(8,128)(2,1)S(1)}, bf16[128,256]{1,0:T(8,128)(2,1)S(1)}, u32[]{:S(2)}, u32[]{:S(2)}) collective-permute-start(bf16[128,256]{1,0:T(8,128)(2,1)S(1)} %get-tuple-element.15.refs_4_), channel_id=1, source_target_pairs={{0,64},{1,65},{2,66},{3,67},{4,68},{5,69},{6,70},{7,71},{8,72},{9,... | collective-permute-start | bytes 196616 | tf_op jit(solution)/shard_map/ppermute | solution.py:53
  99.4 2.9 %collective-permute-done.10 = bf16[192,1024]{1,0:T(8,128)(2,1)S(1)} collective-permute-done((bf16[192,1024]{1,0:T(8,128)(2,1)S(1)}, bf16[192,1024]{1,0:T(8,128)(2,1)S(1)}, u32[]{:S(2)}, u32[]{:S(2)}) %collective-permute-start.10) | collective-permute-done | bytes 393248 | tf_op jit(solution)/shard_map/ppermute | solution.py:53
  102.2 2.2 %fusion.4 = (bf16[192,1024]{1,0:T(8,128)(2,1)S(1)}, bf16[1,192,1024]{2,1,0:T(8,128)(2,1)}) fusion(bf16[192,1024]{1,0:T(8,128)(2,1)S(1)} %copy-done.5, bf16[192,1024]{1,0:T(8,128)(2,1)S(1)} %collective-permute-done.10, bf16[192,1024]{1,0:T(8,128)(2,1)S(1)} %add_convert_fusion.1, bf16[1,192,1024]{2,1,0:T(8,128)(2,1)S(1)} %copy-done.4, ...), kind=kLoop, calls=%fused_computation.8 | loop fusion | flops 3932160 | bytes 2752516 | tf_op jit(solution)/shard_map/convert_element_type | solution.py:275
  (31 shorter events, 5.6 us)
Async XLA Ops:
  0.6 10.0 %copy-start = (bf16[128,6144]{1,0:T(8,128)(2,1)S(1)}, bf16[128,6144]{1,0:T(8,128)(2,1)}, u32[]{:S(2)}) copy-start(bf16[128,6144]{1,0:T(8,128)(2,1)} %refs_0_.2) | copy-start | bytes 4718596
  0.6 0.8 copy-start.2
  2.8 10.4 %collective-permute-start.3 = (bf16[192,128]{1,0:T(8,128)(2,1)S(1)}, bf16[192,128]{1,0:T(8,128)(2,1)S(1)}, u32[]{:S(2)}, u32[]{:S(2)}) collective-permute-start(bf16[192,128]{1,0:T(8,128)(2,1)S(1)} %get-tuple-element.11), channel_id=1, source_target_pairs={{0,1},{1,0},{2,3},{3,2},{4,5},{5,4},{6,7},{7,6},{8,9},{9,8},{10,11... | collective-permute-start | bytes 147464 | tf_op jit(solution)/shard_map/ppermute | solution.py:53
  13.2 42.8 %copy-start.4 = (bf16[1,192,1024]{2,1,0:T(8,128)(2,1)S(1)}, bf16[1,192,1024]{2,1,0:T(8,128)(2,1)}, u32[]{:S(2)}) copy-start(bf16[1,192,1024]{2,1,0:T(8,128)(2,1)} %param.7) | copy-start | bytes 1179652
  13.2 56.5 %collective-permute-start.4 = (bf16[128,6144]{1,0:T(8,128)(2,1)S(1)}, bf16[128,6144]{1,0:T(8,128)(2,1)S(1)}, u32[]{:S(2)}, u32[]{:S(2)}) collective-permute-start(bf16[128,6144]{1,0:T(8,128)(2,1)S(1)} %shard_map.77), channel_id=1, source_target_pairs={{0,64},{1,65},{2,66},{3,67},{4,68},{5,69},{6,70},{7,71},{8,72},{9,... | collective-permute-start | bytes 4718600 | tf_op jit(solution)/shard_map/ppermute | solution.py:53
  15.3 54.5 %collective-permute-start.5 = (bf16[128,6144]{1,0:T(8,128)(2,1)S(1)}, bf16[128,6144]{1,0:T(8,128)(2,1)S(1)}, u32[]{:S(2)}, u32[]{:S(2)}) collective-permute-start(bf16[128,6144]{1,0:T(8,128)(2,1)S(1)} %shard_map.77), channel_id=1, source_target_pairs={{0,128},{1,129},{2,130},{3,131},{4,132},{5,133},{6,134},{7,135},{8... | collective-permute-start | bytes 4718600 | tf_op jit(solution)/shard_map/ppermute | solution.py:53
  17.2 52.5 %collective-permute-start.6 = (bf16[128,6144]{1,0:T(8,128)(2,1)S(1)}, bf16[128,6144]{1,0:T(8,128)(2,1)S(1)}, u32[]{:S(2)}, u32[]{:S(2)}) collective-permute-start(bf16[128,6144]{1,0:T(8,128)(2,1)S(1)} %shard_map.77), channel_id=1, source_target_pairs={{0,192},{1,193},{2,194},{3,195},{4,196},{5,197},{6,198},{7,199},{8... | collective-permute-start | bytes 4718600 | tf_op jit(solution)/shard_map/ppermute | solution.py:53
  52.7 15.1 %collective-permute-start.7 = (bf16[2,4,384,128]{3,2,1,0:T(8,128)(2,1)S(1)}, bf16[2,4,384,128]{3,2,1,0:T(8,128)(2,1)S(1)}, u32[]{:S(2)}, u32[]{:S(2)}) collective-permute-start(bf16[2,4,384,128]{3,2,1,0:T(8,128)(2,1)S(1)} %bitcast.15), channel_id=1, source_target_pairs={{0,2},{1,3},{2,4},{3,5},{4,6},{5,7},{6,8},{7,9},{8,10},{9,11},{10,... | collective-permute-start | bytes 2359304 | tf_op jit(solution)/shard_map/ppermute | solution.py:53
  56.0 3.6 %collective-permute-start = (bf16[192,1024]{1,0:T(8,128)(2,1)S(1)}, bf16[192,1024]{1,0:T(8,128)(2,1)S(1)}, u32[]{:S(2)}, u32[]{:S(2)}) collective-permute-start(bf16[192,1024]{1,0:T(8,128)(2,1)S(1)} %bitcast.22), channel_id=1, source_target_pairs={{0,32},{1,33},{2,34},{3,35},{4,36},{5,37},{6,38},{7,39},{8,40},{9,... | collective-permute-start | bytes 1179656 | tf_op jit(solution)/shard_map/ppermute | solution.py:53
  59.7 14.6 %collective-permute-start.1 = (bf16[192,1024]{1,0:T(8,128)(2,1)S(1)}, bf16[192,1024]{1,0:T(8,128)(2,1)S(1)}, u32[]{:S(2)}, u32[]{:S(2)}) collective-permute-start(bf16[192,1024]{1,0:T(8,128)(2,1)S(1)} %fusion), channel_id=1, source_target_pairs={{0,128},{1,129},{2,130},{3,131},{4,132},{5,133},{6,134},{7,135},{8... | collective-permute-start | bytes 1179656 | tf_op jit(solution)/shard_map/ppermute | solution.py:53
  67.8 15.2 %collective-permute-start.8 = (bf16[2,4,384,128]{3,2,1,0:T(8,128)(2,1)S(1)}, bf16[2,4,384,128]{3,2,1,0:T(8,128)(2,1)S(1)}, u32[]{:S(2)}, u32[]{:S(2)}) collective-permute-start(bf16[2,4,384,128]{3,2,1,0:T(8,128)(2,1)S(1)} %collective-permute-done.7.value_ref.refs_5_), channel_id=1, source_target_pairs={{0,32},{1,33},{2,34},{3,35},{4,36},{5,37},{6,38},{7,39},{8,40},{9,... | collective-permute-start | bytes 2359304 | tf_op jit(solution)/shard_map/ppermute | solution.py:53
  69.8 10.9 %collective-permute-start.9 = (bf16[4,384,128]{2,1,0:T(8,128)(2,1)S(1)}, bf16[4,384,128]{2,1,0:T(8,128)(2,1)S(1)}, u32[]{:S(2)}, u32[]{:S(2)}) collective-permute-start(bf16[4,384,128]{2,1,0:T(8,128)(2,1)S(1)} %shard_map.79), channel_id=1, source_target_pairs={{0,2},{1,3},{2,4},{3,5},{4,6},{5,7},{6,8},{7,9},{8,10},{9,11},{10,... | collective-permute-start | bytes 1179656 | tf_op jit(solution)/shard_map/ppermute | solution.py:53
  74.4 12.2 %collective-permute-start.2 = (bf16[192,1024]{1,0:T(8,128)(2,1)S(1)}, bf16[192,1024]{1,0:T(8,128)(2,1)S(1)}, u32[]{:S(2)}, u32[]{:S(2)}) collective-permute-start(bf16[192,1024]{1,0:T(8,128)(2,1)S(1)} %add_convert_fusion.2.refs_0_), channel_id=1, source_target_pairs={{0,64},{1,65},{2,66},{3,67},{4,68},{5,69},{6,70},{7,71},{8,72},{9,... | collective-permute-start | bytes 1179656 | tf_op jit(solution)/shard_map/ppermute | solution.py:53
  86.7 3.1 %copy-start.3 = (s32[6]{0:T(128)S(1)}, s32[6]{0:T(128)}, u32[]{:S(2)}) copy-start(s32[6]{0:T(128)} %fragment_ref.1) | copy-start | bytes 76
  86.7 15.6 %copy-start.5 = (bf16[192,1024]{1,0:T(8,128)(2,1)S(1)}, bf16[192,1024]{1,0:T(8,128)(2,1)}, u32[]{:S(2)}) copy-start(bf16[192,1024]{1,0:T(8,128)(2,1)} %param.6) | copy-start | bytes 1179652
  86.8 15.4 %collective-permute-start.10 = (bf16[192,1024]{1,0:T(8,128)(2,1)S(1)}, bf16[192,1024]{1,0:T(8,128)(2,1)S(1)}, u32[]{:S(2)}, u32[]{:S(2)}) collective-permute-start(bf16[192,1024]{1,0:T(8,128)(2,1)S(1)} %add_convert_fusion.1), channel_id=1, source_target_pairs={{0,256},{1,257},{2,258},{3,259},{4,260},{5,261},{6,262},{7,263},{8... | collective-permute-start | bytes 1179656 | tf_op jit(solution)/shard_map/ppermute | solution.py:53
  89.9 14.6 %collective-permute-start.11 = (bf16[128,256]{1,0:T(8,128)(2,1)S(1)}, bf16[128,256]{1,0:T(8,128)(2,1)S(1)}, u32[]{:S(2)}, u32[]{:S(2)}) collective-permute-start(bf16[128,256]{1,0:T(8,128)(2,1)S(1)} %get-tuple-element.13.refs_2_), channel_id=1, source_target_pairs={{0,192},{1,193},{2,194},{3,195},{4,196},{5,197},{6,198},{7,199},{8... | collective-permute-start | bytes 196616 | tf_op jit(solution)/shard_map/ppermute | solution.py:53
  91.8 12.6 %collective-permute-start.12 = (bf16[128,256]{1,0:T(8,128)(2,1)S(1)}, bf16[128,256]{1,0:T(8,128)(2,1)S(1)}, u32[]{:S(2)}, u32[]{:S(2)}) collective-permute-start(bf16[128,256]{1,0:T(8,128)(2,1)S(1)} %get-tuple-element.14.refs_3_), channel_id=1, source_target_pairs={{0,128},{1,129},{2,130},{3,131},{4,132},{5,133},{6,134},{7,135},{8... | collective-permute-start | bytes 196616 | tf_op jit(solution)/shard_map/ppermute | solution.py:53
  97.4 7.4 %collective-permute-start.13 = (bf16[128,256]{1,0:T(8,128)(2,1)S(1)}, bf16[128,256]{1,0:T(8,128)(2,1)S(1)}, u32[]{:S(2)}, u32[]{:S(2)}) collective-permute-start(bf16[128,256]{1,0:T(8,128)(2,1)S(1)} %get-tuple-element.15.refs_4_), channel_id=1, source_target_pairs={{0,64},{1,65},{2,66},{3,67},{4,68},{5,69},{6,70},{7,71},{8,72},{9,... | collective-permute-start | bytes 196616 | tf_op jit(solution)/shard_map/ppermute | solution.py:53
  104.5 1.1 %copy-start.1 = (bf16[192,1024]{1,0:T(8,128)(2,1)}, bf16[192,1024]{1,0:T(8,128)(2,1)S(1)}, u32[]{:S(2)}) copy-start(bf16[192,1024]{1,0:T(8,128)(2,1)S(1)} %get-tuple-element.19.refs_4_) | copy-start | bytes 1179652

commit v4 on v3

--- a/solution.py
+++ b/solution.py
@@ -221,7 +221,7 @@
         in_specs=[WHOLE] * CHIPS + [ANY],
         out_specs=WHOLE,
         compiler_params=pltpu.CompilerParams(vmem_limit_bytes=4 << 20),
-    )(*in_vmem(*results), after)
+    )(*in_vmem(*results), *in_hbm(after))
 
 
 def from_beside(at):
@@ -257,22 +257,43 @@
     total, other = gate((total, other), outs[1:])
     total = rounded_sum(total, other)
     results = [outs[0]] + [permute(outs[step], in_group(-step)) for step in (1, 2, 3)]
-    total = rounded_sum(total, permute(total, flip("xh")))
-    return results, total
+    return results, total, permute(total, flip("xh"))
+
+
+def outer_step(weights, momentum, grad, total, other, fragment):
+    rows, cols = grad.shape
+    steps = 2
+    replicas = lax.axis_size(REP)
+
+    def kernel(fragment_ref, weights_ref, momentum_ref, grad_ref, total_ref, other_ref, blended_ref, velocity_ref):
+        del fragment_ref
+        averaged = (total_ref[...].astype(jnp.float32) + other_ref[...].astype(jnp.float32)) / replicas
+        velocity = MU * momentum_ref[...].astype(jnp.float32) + averaged
+        synced = weights_ref[0].astype(jnp.float32)
+        outer_weights = synced - OUTER_LR * (averaged + MU * velocity)
+        inner_weights = synced - grad_ref[...].astype(jnp.float32)
+        blended = MIX * inner_weights + (1.0 - MIX) * outer_weights
+        blended_ref[...] = blended.astype(blended_ref.dtype)
+        velocity_ref[...] = velocity.astype(velocity_ref.dtype)
+
+    block = pl.BlockSpec((rows // steps, cols), lambda n, fragment_ref: (n, 0))
+    layer = pl.BlockSpec((1, rows // steps, cols), lambda n, fragment_ref: (fragment_ref[0], n, 0))
+    return pl.pallas_call(
+        kernel,
+        grid_spec=pltpu.PrefetchScalarGridSpec(
+            num_scalar_prefetch=1,
+            grid=(steps,),
+            in_specs=[layer] + [block] * 4,
+            out_specs=[block] * 2,
+        ),
+        out_shape=[pltpu.HBM(grad.shape, grad.dtype)] * 2,
+        compiler_params=pltpu.CompilerParams(vmem_limit_bytes=12 << 20),
+    )(fragment, weights, momentum, grad, total, other)
 
 
 def per_device(weights, momentum, pseudo_grad, tokens, fragment):
-    results, total = exchange(weights, tokens, pseudo_grad[0], fragment)
-    synced = lax.dynamic_index_in_dim(weights, fragment[0], 0, keepdims=False)
-    replicas = lax.axis_size(REP)
-    own_grad = pseudo_grad[0].astype(jnp.float32)
-    averaged = total.astype(jnp.float32) / replicas
-    velocity = MU * momentum.astype(jnp.float32) + averaged
-    synced_wide = synced.astype(jnp.float32)
-    outer_weights = synced_wide - OUTER_LR * (averaged + MU * velocity)
-    inner_weights = synced_wide - own_grad
-    blended = (MIX * inner_weights + (1.0 - MIX) * outer_weights).astype(jnp.bfloat16)
-    new_momentum = velocity.astype(jnp.bfloat16)
+    results, total, other = exchange(weights, tokens, pseudo_grad[0], fragment)
+    blended, new_momentum = outer_step(weights, momentum, pseudo_grad[0], total, other, fragment)
     return (blended[None], new_momentum, assemble(results, new_momentum))
 
 

time: 106 us -> 106 us (level)
  other arithmetic: 2.61 us -> 0.4 us
  Pallas kernels: 5.81 us -> 7.61 us
    convert_element_type x1 -> x0, other arithmetic: 2.21 us -> none  [per_device(): new_momentum = velocity.astype(jnp.bfloat16)]
    pallas_call x0 -> x1, Pallas kernels: none -> 1.8 us  [outer_step(): pl.pallas_call(kernel, grid_spec=pltpu.PrefetchScalarGridSpec(num_scalar_...]
  transfers between devices with their start and end apart: 14 -> 14, of which waited for: 7 -> 7; matrix products, arithmetic and copies ran while one was open for 2% -> 0% of each run, Pallas kernels for 3% -> 5%
where the time goes in v4:
time: 106 us; the launch traced here: 105 us
  starting transfers between devices  42.8 us (40%)
  blocking collectives  32.7 us (31%)
  waiting for transfers between devices  20.1 us (19%)
  Pallas kernels  7.61 us (7%)
    ppermute x14, starting transfers between devices, permute(): return lax.ppermute(value, AXES, pairs)  42.8 us
    all_gather x1, blocking collectives, exchange(): gathered = lax.all_gather(lay(own, partner), 'zh', axis=0, tiled=False)  28 us
    ppermute x14, waiting for transfers between devices, permute(): return lax.ppermute(value, AXES, pairs)  20.1 us
    pallas_call x1, Pallas kernels, multiply(): pl.pallas_call(kernel, grid=(steps,), out_shape=(vmem_like(shape),) * CHI...  3.61 us
    all_gather x1, blocking collectives, exchange(): here = lax.all_gather(gathered, 'core', axis=0, tiled=False)  2.36 us
    all_gather x1, blocking collectives, exchange(): far = lax.all_gather(far, 'core', axis=0, tiled=False)  2.36 us
  transfers between devices with their start and end apart: 14, of which 7 were waited for; matrix products, arithmetic and copies ran while one was open for 0% of the time, Pallas kernels for 5%

profile of v4, /device:TPU:2, one launch (start us, length us, event | category | flops | bytes accessed | tf_op | source)
XLA Modules:
  0.0 105.5 jit_solution(12632867467361971892)
XLA Ops:
  2.8 7.8 %collective-permute-start.3 = (bf16[192,128]{1,0:T(8,128)(2,1)S(1)}, bf16[192,128]{1,0:T(8,128)(2,1)S(1)}, u32[]{:S(2)}, u32[]{:S(2)}) collective-permute-start(bf16[192,128]{1,0:T(8,128)(2,1)S(1)} %get-tuple-element.13), channel_id=1, source_target_pairs={{0,1},{1,0},{2,3},{3,2},{4,5},{5,4},{6,7},{7,6},{8,9},{9,8},{10,11... | collective-permute-start | bytes 147464 | tf_op jit(solution)/shard_map/ppermute | solution.py:53
  10.8 2.4 %collective-permute-done.3.refs_1_.partner_ref = bf16[192,128]{1,0:T(8,128)(2,1)S(1)} collective-permute-done((bf16[192,128]{1,0:T(8,128)(2,1)S(1)}, bf16[192,128]{1,0:T(8,128)(2,1)S(1)}, u32[]{:S(2)}, u32[]{:S(2)}) %collective-permute-start.3) | collective-permute-done | bytes 49184 | tf_op jit(solution)/shard_map/ppermute | solution.py:53
  13.2 2.0 %collective-permute-start.4 = (bf16[128,6144]{1,0:T(8,128)(2,1)S(1)}, bf16[128,6144]{1,0:T(8,128)(2,1)S(1)}, u32[]{:S(2)}, u32[]{:S(2)}) collective-permute-start(bf16[128,6144]{1,0:T(8,128)(2,1)S(1)} %shard_map.77), channel_id=1, source_target_pairs={{0,64},{1,65},{2,66},{3,67},{4,68},{5,69},{6,70},{7,71},{8,72},{9,... | collective-permute-start | bytes 4718600 | tf_op jit(solution)/shard_map/ppermute | solution.py:53
  15.3 2.0 %collective-permute-start.5 = (bf16[128,6144]{1,0:T(8,128)(2,1)S(1)}, bf16[128,6144]{1,0:T(8,128)(2,1)S(1)}, u32[]{:S(2)}, u32[]{:S(2)}) collective-permute-start(bf16[128,6144]{1,0:T(8,128)(2,1)S(1)} %shard_map.77), channel_id=1, source_target_pairs={{0,128},{1,129},{2,130},{3,131},{4,132},{5,133},{6,134},{7,135},{8... | collective-permute-start | bytes 4718600 | tf_op jit(solution)/shard_map/ppermute | solution.py:53
  17.2 5.1 %collective-permute-start.6 = (bf16[128,6144]{1,0:T(8,128)(2,1)S(1)}, bf16[128,6144]{1,0:T(8,128)(2,1)S(1)}, u32[]{:S(2)}, u32[]{:S(2)}) collective-permute-start(bf16[128,6144]{1,0:T(8,128)(2,1)S(1)} %shard_map.77), channel_id=1, source_target_pairs={{0,192},{1,193},{2,194},{3,195},{4,196},{5,197},{6,198},{7,199},{8... | collective-permute-start | bytes 4718600 | tf_op jit(solution)/shard_map/ppermute | solution.py:53
  22.4 28.0 %all-gather = bf16[1536,128]{1,0:T(8,128)(2,1)S(1)} all-gather(bf16[384,128]{1,0:T(8,128)(2,1)S(1)} %shard_map.78), channel_id=2, replica_groups=mesh['xh'=2,'y'=4,'core'=2,'zh'=4,'zl'=4,'xl'=2] {'zh'}, dimensions={0}, use_global_device_ids=true | all-gather | bytes 491520 | tf_op jit(solution)/shard_map/all_gather | solution.py:246
  50.4 2.4 %all-gather.1 = bf16[8,384,128]{2,1,0:T(8,128)(2,1)S(1)} all-gather(bf16[4,384,128]{2,1,0:T(8,128)(2,1)S(1)} %bitcast.11), channel_id=3, replica_groups=mesh['xh'=2,'y'=4,'core'=2,'zh'=4,'zl'=4,'xl'=2] {'core'}, dimensions={0}, use_global_device_ids=true | all-gather | bytes 1179648 | tf_op jit(solution)/shard_map/all_gather | solution.py:247
  52.7 3.2 %collective-permute-start.7 = (bf16[2,4,384,128]{3,2,1,0:T(8,128)(2,1)S(1)}, bf16[2,4,384,128]{3,2,1,0:T(8,128)(2,1)S(1)}, u32[]{:S(2)}, u32[]{:S(2)}) collective-permute-start(bf16[2,4,384,128]{3,2,1,0:T(8,128)(2,1)S(1)} %bitcast.6), channel_id=1, source_target_pairs={{0,2},{1,3},{2,4},{3,5},{4,6},{5,7},{6,8},{7,9},{8,10},{9,11},{10,... | collective-permute-start | bytes 2359304 | tf_op jit(solution)/shard_map/ppermute | solution.py:53
  56.0 1.9 %collective-permute-start = (bf16[192,1024]{1,0:T(8,128)(2,1)S(1)}, bf16[192,1024]{1,0:T(8,128)(2,1)S(1)}, u32[]{:S(2)}, u32[]{:S(2)}) collective-permute-start(bf16[192,1024]{1,0:T(8,128)(2,1)S(1)} %bitcast.9), channel_id=1, source_target_pairs={{0,32},{1,33},{2,34},{3,35},{4,36},{5,37},{6,38},{7,39},{8,40},{9,... | collective-permute-start | bytes 1179656 | tf_op jit(solution)/shard_map/ppermute | solution.py:53
  59.7 1.9 %collective-permute-start.1 = (bf16[192,1024]{1,0:T(8,128)(2,1)S(1)}, bf16[192,1024]{1,0:T(8,128)(2,1)S(1)}, u32[]{:S(2)}, u32[]{:S(2)}) collective-permute-start(bf16[192,1024]{1,0:T(8,128)(2,1)S(1)} %add_convert_fusion.2), channel_id=1, source_target_pairs={{0,128},{1,129},{2,130},{3,131},{4,132},{5,133},{6,134},{7,135},{8... | collective-permute-start | bytes 1179656 | tf_op jit(solution)/shard_map/ppermute | solution.py:53
  61.7 6.1 %collective-permute-done.7.value_ref.refs_5_ = bf16[2,4,384,128]{3,2,1,0:T(8,128)(2,1)S(1)} collective-permute-done((bf16[2,4,384,128]{3,2,1,0:T(8,128)(2,1)S(1)}, bf16[2,4,384,128]{3,2,1,0:T(8,128)(2,1)S(1)}, u32[]{:S(2)}, u32[]{:S(2)}) %collective-permute-start.7) | collective-permute-done | bytes 786464 | tf_op jit(solution)/shard_map/ppermute | solution.py:53
  67.8 1.9 %collective-permute-start.8 = (bf16[2,4,384,128]{3,2,1,0:T(8,128)(2,1)S(1)}, bf16[2,4,384,128]{3,2,1,0:T(8,128)(2,1)S(1)}, u32[]{:S(2)}, u32[]{:S(2)}) collective-permute-start(bf16[2,4,384,128]{3,2,1,0:T(8,128)(2,1)S(1)} %collective-permute-done.7.value_ref.refs_5_), channel_id=1, source_target_pairs={{0,32},{1,33},{2,34},{3,35},{4,36},{5,37},{6,38},{7,39},{8,40},{9,... | collective-permute-start | bytes 2359304 | tf_op jit(solution)/shard_map/ppermute | solution.py:53
  69.8 2.0 %collective-permute-start.9 = (bf16[4,384,128]{2,1,0:T(8,128)(2,1)S(1)}, bf16[4,384,128]{2,1,0:T(8,128)(2,1)S(1)}, u32[]{:S(2)}, u32[]{:S(2)}) collective-permute-start(bf16[4,384,128]{2,1,0:T(8,128)(2,1)S(1)} %shard_map.79), channel_id=1, source_target_pairs={{0,2},{1,3},{2,4},{3,5},{4,6},{5,7},{6,8},{7,9},{8,10},{9,11},{10,... | collective-permute-start | bytes 1179656 | tf_op jit(solution)/shard_map/ppermute | solution.py:53
  71.9 2.4 %collective-permute-done.1 = bf16[192,1024]{1,0:T(8,128)(2,1)S(1)} collective-permute-done((bf16[192,1024]{1,0:T(8,128)(2,1)S(1)}, bf16[192,1024]{1,0:T(8,128)(2,1)S(1)}, u32[]{:S(2)}, u32[]{:S(2)}) %collective-permute-start.1) | collective-permute-done | bytes 393248 | tf_op jit(solution)/shard_map/ppermute | solution.py:53
  74.4 2.5 %collective-permute-start.2 = (bf16[192,1024]{1,0:T(8,128)(2,1)S(1)}, bf16[192,1024]{1,0:T(8,128)(2,1)S(1)}, u32[]{:S(2)}, u32[]{:S(2)}) collective-permute-start(bf16[192,1024]{1,0:T(8,128)(2,1)S(1)} %add_convert_fusion.1.refs_0_), channel_id=1, source_target_pairs={{0,64},{1,65},{2,66},{3,67},{4,68},{5,69},{6,70},{7,71},{8,72},{9,... | collective-permute-start | bytes 1179656 | tf_op jit(solution)/shard_map/ppermute | solution.py:53
  76.9 3.8 %collective-permute-done.9 = bf16[4,384,128]{2,1,0:T(8,128)(2,1)S(1)} collective-permute-done((bf16[4,384,128]{2,1,0:T(8,128)(2,1)S(1)}, bf16[4,384,128]{2,1,0:T(8,128)(2,1)S(1)}, u32[]{:S(2)}, u32[]{:S(2)}) %collective-permute-start.9) | collective-permute-done | bytes 393248 | tf_op jit(solution)/shard_map/ppermute | solution.py:53
  80.7 2.4 %all-gather.2 = bf16[8,384,128]{2,1,0:T(8,128)(2,1)S(1)} all-gather(bf16[4,384,128]{2,1,0:T(8,128)(2,1)S(1)} %collective-permute-done.9), channel_id=4, replica_groups=mesh['xh'=2,'y'=4,'core'=2,'zh'=4,'zl'=4,'xl'=2] {'core'}, dimensions={0}, use_global_device_ids=true | all-gather | bytes 1179648 | tf_op jit(solution)/shard_map/all_gather | solution.py:253
  83.0 3.6 %shard_map.80 = (bf16[128,256]{1,0:T(8,128)(2,1)S(1)}, bf16[128,256]{1,0:T(8,128)(2,1)S(1)}, bf16[128,256]{1,0:T(8,128)(2,1)S(1)}, bf16[128,256]{1,0:T(8,128)(2,1)S(1)}) custom-call(bf16[128,6144]{1,0:T(8,128)(2,1)S(1)} %copy-done.1, bf16[128,6144]{1,0:T(8,128)(2,1)S(1)} %collective-permute-done.4.refs_0_.refs_1_, ...), custom_call_target="tpu_custom_call" | custom-call | flops 1610612736 | bytes 9437184 | tf_op jit(solution)/shard_map/pallas_call | solution.py:192
  86.9 2.9 %collective-permute-start.10 = (bf16[192,1024]{1,0:T(8,128)(2,1)S(1)}, bf16[192,1024]{1,0:T(8,128)(2,1)S(1)}, u32[]{:S(2)}, u32[]{:S(2)}) collective-permute-start(bf16[192,1024]{1,0:T(8,128)(2,1)S(1)} %add_convert_fusion.total_ref), channel_id=1, source_target_pairs={{0,256},{1,257},{2,258},{3,259},{4,260},{5,261},{6,262},{7,263},{8... | collective-permute-start | bytes 1179656 | tf_op jit(solution)/shard_map/ppermute | solution.py:53
  89.8 1.9 %collective-permute-start.11 = (bf16[128,256]{1,0:T(8,128)(2,1)S(1)}, bf16[128,256]{1,0:T(8,128)(2,1)S(1)}, u32[]{:S(2)}, u32[]{:S(2)}) collective-permute-start(bf16[128,256]{1,0:T(8,128)(2,1)S(1)} %get-tuple-element.15.refs_2_), channel_id=1, source_target_pairs={{0,192},{1,193},{2,194},{3,195},{4,196},{5,197},{6,198},{7,199},{8... | collective-permute-start | bytes 196616 | tf_op jit(solution)/shard_map/ppermute | solution.py:53
  91.7 5.6 %collective-permute-start.12 = (bf16[128,256]{1,0:T(8,128)(2,1)S(1)}, bf16[128,256]{1,0:T(8,128)(2,1)S(1)}, u32[]{:S(2)}, u32[]{:S(2)}) collective-permute-start(bf16[128,256]{1,0:T(8,128)(2,1)S(1)} %get-tuple-element.16.refs_3_), channel_id=1, source_target_pairs={{0,128},{1,129},{2,130},{3,131},{4,132},{5,133},{6,134},{7,135},{8... | collective-permute-start | bytes 196616 | tf_op jit(solution)/shard_map/ppermute | solution.py:53
  97.3 1.9 %collective-permute-start.13 = (bf16[128,256]{1,0:T(8,128)(2,1)S(1)}, bf16[128,256]{1,0:T(8,128)(2,1)S(1)}, u32[]{:S(2)}, u32[]{:S(2)}) collective-permute-start(bf16[128,256]{1,0:T(8,128)(2,1)S(1)} %get-tuple-element.17.refs_4_), channel_id=1, source_target_pairs={{0,64},{1,65},{2,66},{3,67},{4,68},{5,69},{6,70},{7,71},{8,72},{9,... | collective-permute-start | bytes 196616 | tf_op jit(solution)/shard_map/ppermute | solution.py:53
  99.3 3.0 %collective-permute-done.10.other_ref = bf16[192,1024]{1,0:T(8,128)(2,1)S(1)} collective-permute-done((bf16[192,1024]{1,0:T(8,128)(2,1)S(1)}, bf16[192,1024]{1,0:T(8,128)(2,1)S(1)}, u32[]{:S(2)}, u32[]{:S(2)}) %collective-permute-start.10) | collective-permute-done | bytes 393248 | tf_op jit(solution)/shard_map/ppermute | solution.py:53
  102.3 1.8 %shard_map.82 = (bf16[192,1024]{1,0:T(8,128)(2,1)}, bf16[192,1024]{1,0:T(8,128)(2,1)}) custom-call(s32[6]{0:T(128)S(1)} %copy-done.5, bf16[6,192,1024]{2,1,0:T(8,128)(2,1)S(1)} %copy-done, bf16[192,1024]{1,0:T(8,128)(2,1)S(1)} %copy-done.3, bf16[192,1024]{1,0:T(8,128)(2,1)S(1)} %bitcast.10, bf16[192,1024]{1,0:T(8,128)(2,1)S(1)} %add_convert_fusion.total_ref, ...), custom_call_target="tpu_custom_call" | custom-call | tf_op jit(solution)/shard_map/pallas_call | solution.py:281
  (31 shorter events, 5.9 us)
Async XLA Ops:
  0.6 10.0 %copy-start.1 = (bf16[128,6144]{1,0:T(8,128)(2,1)S(1)}, bf16[128,6144]{1,0:T(8,128)(2,1)}, u32[]{:S(2)}) copy-start(bf16[128,6144]{1,0:T(8,128)(2,1)} %refs_0_.2) | copy-start | bytes 4718596
  0.6 0.8 copy-start.4
  2.8 10.4 %collective-permute-start.3 = (bf16[192,128]{1,0:T(8,128)(2,1)S(1)}, bf16[192,128]{1,0:T(8,128)(2,1)S(1)}, u32[]{:S(2)}, u32[]{:S(2)}) collective-permute-start(bf16[192,128]{1,0:T(8,128)(2,1)S(1)} %get-tuple-element.13), channel_id=1, source_target_pairs={{0,1},{1,0},{2,3},{3,2},{4,5},{5,4},{6,7},{7,6},{8,9},{9,8},{10,11... | collective-permute-start | bytes 147464 | tf_op jit(solution)/shard_map/ppermute | solution.py:53
  13.2 42.8 %copy-start.2 = (bf16[1,192,1024]{2,1,0:T(8,128)(2,1)S(1)}, bf16[1,192,1024]{2,1,0:T(8,128)(2,1)}, u32[]{:S(2)}) copy-start(bf16[1,192,1024]{2,1,0:T(8,128)(2,1)} %param.7) | copy-start | bytes 1179652
  13.2 56.5 %collective-permute-start.4 = (bf16[128,6144]{1,0:T(8,128)(2,1)S(1)}, bf16[128,6144]{1,0:T(8,128)(2,1)S(1)}, u32[]{:S(2)}, u32[]{:S(2)}) collective-permute-start(bf16[128,6144]{1,0:T(8,128)(2,1)S(1)} %shard_map.77), channel_id=1, source_target_pairs={{0,64},{1,65},{2,66},{3,67},{4,68},{5,69},{6,70},{7,71},{8,72},{9,... | collective-permute-start | bytes 4718600 | tf_op jit(solution)/shard_map/ppermute | solution.py:53
  15.3 54.5 %collective-permute-start.5 = (bf16[128,6144]{1,0:T(8,128)(2,1)S(1)}, bf16[128,6144]{1,0:T(8,128)(2,1)S(1)}, u32[]{:S(2)}, u32[]{:S(2)}) collective-permute-start(bf16[128,6144]{1,0:T(8,128)(2,1)S(1)} %shard_map.77), channel_id=1, source_target_pairs={{0,128},{1,129},{2,130},{3,131},{4,132},{5,133},{6,134},{7,135},{8... | collective-permute-start | bytes 4718600 | tf_op jit(solution)/shard_map/ppermute | solution.py:53
  17.2 52.5 %collective-permute-start.6 = (bf16[128,6144]{1,0:T(8,128)(2,1)S(1)}, bf16[128,6144]{1,0:T(8,128)(2,1)S(1)}, u32[]{:S(2)}, u32[]{:S(2)}) collective-permute-start(bf16[128,6144]{1,0:T(8,128)(2,1)S(1)} %shard_map.77), channel_id=1, source_target_pairs={{0,192},{1,193},{2,194},{3,195},{4,196},{5,197},{6,198},{7,199},{8... | collective-permute-start | bytes 4718600 | tf_op jit(solution)/shard_map/ppermute | solution.py:53
  52.7 15.1 %collective-permute-start.7 = (bf16[2,4,384,128]{3,2,1,0:T(8,128)(2,1)S(1)}, bf16[2,4,384,128]{3,2,1,0:T(8,128)(2,1)S(1)}, u32[]{:S(2)}, u32[]{:S(2)}) collective-permute-start(bf16[2,4,384,128]{3,2,1,0:T(8,128)(2,1)S(1)} %bitcast.6), channel_id=1, source_target_pairs={{0,2},{1,3},{2,4},{3,5},{4,6},{5,7},{6,8},{7,9},{8,10},{9,11},{10,... | collective-permute-start | bytes 2359304 | tf_op jit(solution)/shard_map/ppermute | solution.py:53
  56.0 3.6 %collective-permute-start = (bf16[192,1024]{1,0:T(8,128)(2,1)S(1)}, bf16[192,1024]{1,0:T(8,128)(2,1)S(1)}, u32[]{:S(2)}, u32[]{:S(2)}) collective-permute-start(bf16[192,1024]{1,0:T(8,128)(2,1)S(1)} %bitcast.9), channel_id=1, source_target_pairs={{0,32},{1,33},{2,34},{3,35},{4,36},{5,37},{6,38},{7,39},{8,40},{9,... | collective-permute-start | bytes 1179656 | tf_op jit(solution)/shard_map/ppermute | solution.py:53
  59.7 14.6 %collective-permute-start.1 = (bf16[192,1024]{1,0:T(8,128)(2,1)S(1)}, bf16[192,1024]{1,0:T(8,128)(2,1)S(1)}, u32[]{:S(2)}, u32[]{:S(2)}) collective-permute-start(bf16[192,1024]{1,0:T(8,128)(2,1)S(1)} %add_convert_fusion.2), channel_id=1, source_target_pairs={{0,128},{1,129},{2,130},{3,131},{4,132},{5,133},{6,134},{7,135},{8... | collective-permute-start | bytes 1179656 | tf_op jit(solution)/shard_map/ppermute | solution.py:53
  67.8 15.2 %collective-permute-start.8 = (bf16[2,4,384,128]{3,2,1,0:T(8,128)(2,1)S(1)}, bf16[2,4,384,128]{3,2,1,0:T(8,128)(2,1)S(1)}, u32[]{:S(2)}, u32[]{:S(2)}) collective-permute-start(bf16[2,4,384,128]{3,2,1,0:T(8,128)(2,1)S(1)} %collective-permute-done.7.value_ref.refs_5_), channel_id=1, source_target_pairs={{0,32},{1,33},{2,34},{3,35},{4,36},{5,37},{6,38},{7,39},{8,40},{9,... | collective-permute-start | bytes 2359304 | tf_op jit(solution)/shard_map/ppermute | solution.py:53
  69.8 10.9 %collective-permute-start.9 = (bf16[4,384,128]{2,1,0:T(8,128)(2,1)S(1)}, bf16[4,384,128]{2,1,0:T(8,128)(2,1)S(1)}, u32[]{:S(2)}, u32[]{:S(2)}) collective-permute-start(bf16[4,384,128]{2,1,0:T(8,128)(2,1)S(1)} %shard_map.79), channel_id=1, source_target_pairs={{0,2},{1,3},{2,4},{3,5},{4,6},{5,7},{6,8},{7,9},{8,10},{9,11},{10,... | collective-permute-start | bytes 1179656 | tf_op jit(solution)/shard_map/ppermute | solution.py:53
  74.4 12.3 %collective-permute-start.2 = (bf16[192,1024]{1,0:T(8,128)(2,1)S(1)}, bf16[192,1024]{1,0:T(8,128)(2,1)S(1)}, u32[]{:S(2)}, u32[]{:S(2)}) collective-permute-start(bf16[192,1024]{1,0:T(8,128)(2,1)S(1)} %add_convert_fusion.1.refs_0_), channel_id=1, source_target_pairs={{0,64},{1,65},{2,66},{3,67},{4,68},{5,69},{6,70},{7,71},{8,72},{9,... | collective-permute-start | bytes 1179656 | tf_op jit(solution)/shard_map/ppermute | solution.py:53
  83.0 19.2 %copy-start = (bf16[6,192,1024]{2,1,0:T(8,128)(2,1)S(1)}, bf16[6,192,1024]{2,1,0:T(8,128)(2,1)}, u32[]{:S(2)}) copy-start(bf16[6,192,1024]{2,1,0:T(8,128)(2,1)} %weights_ref.3) | copy-start | bytes 7077892
  86.7 15.6 %copy-start.3 = (bf16[192,1024]{1,0:T(8,128)(2,1)S(1)}, bf16[192,1024]{1,0:T(8,128)(2,1)}, u32[]{:S(2)}) copy-start(bf16[192,1024]{1,0:T(8,128)(2,1)} %momentum_ref.1) | copy-start | bytes 1179652
  86.7 15.6 %copy-start.5 = (s32[6]{0:T(128)S(1)}, s32[6]{0:T(128)}, u32[]{:S(2)}) copy-start(s32[6]{0:T(128)} %fragment_ref.3) | copy-start | bytes 76
  86.9 15.4 %collective-permute-start.10 = (bf16[192,1024]{1,0:T(8,128)(2,1)S(1)}, bf16[192,1024]{1,0:T(8,128)(2,1)S(1)}, u32[]{:S(2)}, u32[]{:S(2)}) collective-permute-start(bf16[192,1024]{1,0:T(8,128)(2,1)S(1)} %add_convert_fusion.total_ref), channel_id=1, source_target_pairs={{0,256},{1,257},{2,258},{3,259},{4,260},{5,261},{6,262},{7,263},{8... | collective-permute-start | bytes 1179656 | tf_op jit(solution)/shard_map/ppermute | solution.py:53
  89.8 14.3 %collective-permute-start.11 = (bf16[128,256]{1,0:T(8,128)(2,1)S(1)}, bf16[128,256]{1,0:T(8,128)(2,1)S(1)}, u32[]{:S(2)}, u32[]{:S(2)}) collective-permute-start(bf16[128,256]{1,0:T(8,128)(2,1)S(1)} %get-tuple-element.15.refs_2_), channel_id=1, source_target_pairs={{0,192},{1,193},{2,194},{3,195},{4,196},{5,197},{6,198},{7,199},{8... | collective-permute-start | bytes 196616 | tf_op jit(solution)/shard_map/ppermute | solution.py:53
  91.7 12.3 %collective-permute-start.12 = (bf16[128,256]{1,0:T(8,128)(2,1)S(1)}, bf16[128,256]{1,0:T(8,128)(2,1)S(1)}, u32[]{:S(2)}, u32[]{:S(2)}) collective-permute-start(bf16[128,256]{1,0:T(8,128)(2,1)S(1)} %get-tuple-element.16.refs_3_), channel_id=1, source_target_pairs={{0,128},{1,129},{2,130},{3,131},{4,132},{5,133},{6,134},{7,135},{8... | collective-permute-start | bytes 196616 | tf_op jit(solution)/shard_map/ppermute | solution.py:53
  97.3 7.4 %collective-permute-start.13 = (bf16[128,256]{1,0:T(8,128)(2,1)S(1)}, bf16[128,256]{1,0:T(8,128)(2,1)S(1)}, u32[]{:S(2)}, u32[]{:S(2)}) collective-permute-start(bf16[128,256]{1,0:T(8,128)(2,1)S(1)} %get-tuple-element.17.refs_4_), channel_id=1, source_target_pairs={{0,64},{1,65},{2,66},{3,67},{4,68},{5,69},{6,70},{7,71},{8,72},{9,... | collective-permute-start | bytes 196616 | tf_op jit(solution)/shard_map/ppermute | solution.py:53

commit v5 on v3

--- a/solution.py
+++ b/solution.py
@@ -170,7 +170,8 @@
         for n, token_ref in enumerate(token_refs):
             part = None
             for ref, place in sets:
-                weight = jnp.concatenate([ref[half, 0] for half in range(halves)], axis=1)
+                at = step if ref is far_ref else 0
+                weight = jnp.concatenate([ref[half, at] for half in range(halves)], axis=1)
                 plane = lax.rem(zl + place, PARTS)
                 if n == 0:
                     plane += step * PARTS
@@ -193,7 +194,7 @@
         kernel,
         grid=(steps,),
         out_shape=(vmem_like(shape),) * CHIPS,
-        in_specs=[WHOLE] + [token_spec] * (CHIPS - 1) + [weight_spec] * 4,
+        in_specs=[WHOLE] + [token_spec] * (CHIPS - 1) + [weight_spec] * 3 + [WHOLE],
         out_specs=(WHOLE,) * CHIPS,
         scratch_shapes=[pltpu.VMEM((CHIPS, *shape), jnp.float32)],
         compiler_params=pltpu.CompilerParams(vmem_limit_bytes=32 << 20),
@@ -202,7 +203,7 @@
             bytes_accessed=2 * (CHIPS * tokens + halves * width) * depth,
             transcendentals=0,
         ),
-    )(*in_vmem(blocks[0]), *blocks[1:], here, mine, theirs, far)
+    )(*in_vmem(blocks[0]), *blocks[1:], here, mine, theirs, *in_vmem(far))
 
 
 def assemble(results, after):

time: 106 us -> 106 us (level)
  no operation moved by 1% of the time
where the time goes in v5:
time: 106 us
  starting transfers between devices  42.8 us (40%)
  blocking collectives  32.7 us (31%)
  waiting for transfers between devices  19.7 us (19%)
  Pallas kernels  5.75 us (5%)
  other arithmetic  2.61 us (2%)
    ppermute x14, starting transfers between devices, permute(): return lax.ppermute(value, AXES, pairs)  42.8 us
    all_gather x1, blocking collectives, exchange(): gathered = lax.all_gather(lay(own, partner), 'zh', axis=0, tiled=False)  28 us
    ppermute x14, waiting for transfers between devices, permute(): return lax.ppermute(value, AXES, pairs)  19.7 us
    pallas_call x1, Pallas kernels, multiply(): pl.pallas_call(kernel, grid=(steps,), out_shape=(vmem_like(shape),) * CHI...  3.55 us
    all_gather x1, blocking collectives, exchange(): here = lax.all_gather(gathered, 'core', axis=0, tiled=False)  2.36 us
    all_gather x1, blocking collectives, exchange(): far = lax.all_gather(far, 'core', axis=0, tiled=False)  2.36 us
    convert_element_type x1, other arithmetic, per_device(): new_momentum = velocity.astype(jnp.bfloat16)  2.21 us
  transfers between devices with their start and end apart: 14, of which 7 were waited for; matrix products, arithmetic and copies ran while one was open for 2% of the time, Pallas kernels for 3%

profile of v5, /device:TPU:2, one launch (start us, length us, event | category | flops | bytes accessed | tf_op | source)
XLA Modules:
  0.0 105.5 jit_solution(6457613855959293067)
XLA Ops:
  2.8 7.8 %collective-permute-start.3 = (bf16[192,128]{1,0:T(8,128)(2,1)S(1)}, bf16[192,128]{1,0:T(8,128)(2,1)S(1)}, u32[]{:S(2)}, u32[]{:S(2)}) collective-permute-start(bf16[192,128]{1,0:T(8,128)(2,1)S(1)} %get-tuple-element.11), channel_id=1, source_target_pairs={{0,1},{1,0},{2,3},{3,2},{4,5},{5,4},{6,7},{7,6},{8,9},{9,8},{10,11... | collective-permute-start | bytes 147464 | tf_op jit(solution)/shard_map/ppermute | solution.py:53
  10.8 2.4 %collective-permute-done.3.refs_1_.partner_ref = bf16[192,128]{1,0:T(8,128)(2,1)S(1)} collective-permute-done((bf16[192,128]{1,0:T(8,128)(2,1)S(1)}, bf16[192,128]{1,0:T(8,128)(2,1)S(1)}, u32[]{:S(2)}, u32[]{:S(2)}) %collective-permute-start.3) | collective-permute-done | bytes 49184 | tf_op jit(solution)/shard_map/ppermute | solution.py:53
  13.2 2.0 %collective-permute-start.4 = (bf16[128,6144]{1,0:T(8,128)(2,1)S(1)}, bf16[128,6144]{1,0:T(8,128)(2,1)S(1)}, u32[]{:S(2)}, u32[]{:S(2)}) collective-permute-start(bf16[128,6144]{1,0:T(8,128)(2,1)S(1)} %shard_map.77), channel_id=1, source_target_pairs={{0,64},{1,65},{2,66},{3,67},{4,68},{5,69},{6,70},{7,71},{8,72},{9,... | collective-permute-start | bytes 4718600 | tf_op jit(solution)/shard_map/ppermute | solution.py:53
  15.3 2.0 %collective-permute-start.5 = (bf16[128,6144]{1,0:T(8,128)(2,1)S(1)}, bf16[128,6144]{1,0:T(8,128)(2,1)S(1)}, u32[]{:S(2)}, u32[]{:S(2)}) collective-permute-start(bf16[128,6144]{1,0:T(8,128)(2,1)S(1)} %shard_map.77), channel_id=1, source_target_pairs={{0,128},{1,129},{2,130},{3,131},{4,132},{5,133},{6,134},{7,135},{8... | collective-permute-start | bytes 4718600 | tf_op jit(solution)/shard_map/ppermute | solution.py:53
  17.2 5.1 %collective-permute-start.6 = (bf16[128,6144]{1,0:T(8,128)(2,1)S(1)}, bf16[128,6144]{1,0:T(8,128)(2,1)S(1)}, u32[]{:S(2)}, u32[]{:S(2)}) collective-permute-start(bf16[128,6144]{1,0:T(8,128)(2,1)S(1)} %shard_map.77), channel_id=1, source_target_pairs={{0,192},{1,193},{2,194},{3,195},{4,196},{5,197},{6,198},{7,199},{8... | collective-permute-start | bytes 4718600 | tf_op jit(solution)/shard_map/ppermute | solution.py:53
  22.4 28.0 %all-gather = bf16[1536,128]{1,0:T(8,128)(2,1)S(1)} all-gather(bf16[384,128]{1,0:T(8,128)(2,1)S(1)} %shard_map.78), channel_id=2, replica_groups=mesh['xh'=2,'y'=4,'core'=2,'zh'=4,'zl'=4,'xl'=2] {'zh'}, dimensions={0}, use_global_device_ids=true | all-gather | bytes 491520 | tf_op jit(solution)/shard_map/all_gather | solution.py:247
  50.4 2.4 %all-gather.1 = bf16[8,384,128]{2,1,0:T(8,128)(2,1)S(1)} all-gather(bf16[4,384,128]{2,1,0:T(8,128)(2,1)S(1)} %bitcast.21), channel_id=3, replica_groups=mesh['xh'=2,'y'=4,'core'=2,'zh'=4,'zl'=4,'xl'=2] {'core'}, dimensions={0}, use_global_device_ids=true | all-gather | bytes 1179648 | tf_op jit(solution)/shard_map/all_gather | solution.py:248
  52.7 3.2 %collective-permute-start.7 = (bf16[2,4,384,128]{3,2,1,0:T(8,128)(2,1)S(1)}, bf16[2,4,384,128]{3,2,1,0:T(8,128)(2,1)S(1)}, u32[]{:S(2)}, u32[]{:S(2)}) collective-permute-start(bf16[2,4,384,128]{3,2,1,0:T(8,128)(2,1)S(1)} %bitcast.15), channel_id=1, source_target_pairs={{0,2},{1,3},{2,4},{3,5},{4,6},{5,7},{6,8},{7,9},{8,10},{9,11},{10,... | collective-permute-start | bytes 2359304 | tf_op jit(solution)/shard_map/ppermute | solution.py:53
  56.0 1.9 %collective-permute-start = (bf16[192,1024]{1,0:T(8,128)(2,1)S(1)}, bf16[192,1024]{1,0:T(8,128)(2,1)S(1)}, u32[]{:S(2)}, u32[]{:S(2)}) collective-permute-start(bf16[192,1024]{1,0:T(8,128)(2,1)S(1)} %bitcast.22), channel_id=1, source_target_pairs={{0,32},{1,33},{2,34},{3,35},{4,36},{5,37},{6,38},{7,39},{8,40},{9,... | collective-permute-start | bytes 1179656 | tf_op jit(solution)/shard_map/ppermute | solution.py:53
  59.7 1.9 %collective-permute-start.1 = (bf16[192,1024]{1,0:T(8,128)(2,1)S(1)}, bf16[192,1024]{1,0:T(8,128)(2,1)S(1)}, u32[]{:S(2)}, u32[]{:S(2)}) collective-permute-start(bf16[192,1024]{1,0:T(8,128)(2,1)S(1)} %fusion), channel_id=1, source_target_pairs={{0,128},{1,129},{2,130},{3,131},{4,132},{5,133},{6,134},{7,135},{8... | collective-permute-start | bytes 1179656 | tf_op jit(solution)/shard_map/ppermute | solution.py:53
  61.7 6.1 %collective-permute-done.7.value_ref.refs_5_ = bf16[2,4,384,128]{3,2,1,0:T(8,128)(2,1)S(1)} collective-permute-done((bf16[2,4,384,128]{3,2,1,0:T(8,128)(2,1)S(1)}, bf16[2,4,384,128]{3,2,1,0:T(8,128)(2,1)S(1)}, u32[]{:S(2)}, u32[]{:S(2)}) %collective-permute-start.7) | collective-permute-done | bytes 786464 | tf_op jit(solution)/shard_map/ppermute | solution.py:53
  67.8 1.9 %collective-permute-start.8 = (bf16[2,4,384,128]{3,2,1,0:T(8,128)(2,1)S(1)}, bf16[2,4,384,128]{3,2,1,0:T(8,128)(2,1)S(1)}, u32[]{:S(2)}, u32[]{:S(2)}) collective-permute-start(bf16[2,4,384,128]{3,2,1,0:T(8,128)(2,1)S(1)} %collective-permute-done.7.value_ref.refs_5_), channel_id=1, source_target_pairs={{0,32},{1,33},{2,34},{3,35},{4,36},{5,37},{6,38},{7,39},{8,40},{9,... | collective-permute-start | bytes 2359304 | tf_op jit(solution)/shard_map/ppermute | solution.py:53
  69.8 2.0 %collective-permute-start.9 = (bf16[4,384,128]{2,1,0:T(8,128)(2,1)S(1)}, bf16[4,384,128]{2,1,0:T(8,128)(2,1)S(1)}, u32[]{:S(2)}, u32[]{:S(2)}) collective-permute-start(bf16[4,384,128]{2,1,0:T(8,128)(2,1)S(1)} %shard_map.79), channel_id=1, source_target_pairs={{0,2},{1,3},{2,4},{3,5},{4,6},{5,7},{6,8},{7,9},{8,10},{9,11},{10,... | collective-permute-start | bytes 1179656 | tf_op jit(solution)/shard_map/ppermute | solution.py:53
  71.9 2.4 %collective-permute-done.1 = bf16[192,1024]{1,0:T(8,128)(2,1)S(1)} collective-permute-done((bf16[192,1024]{1,0:T(8,128)(2,1)S(1)}, bf16[192,1024]{1,0:T(8,128)(2,1)S(1)}, u32[]{:S(2)}, u32[]{:S(2)}) %collective-permute-start.1) | collective-permute-done | bytes 393248 | tf_op jit(solution)/shard_map/ppermute | solution.py:53
  74.4 2.5 %collective-permute-start.2 = (bf16[192,1024]{1,0:T(8,128)(2,1)S(1)}, bf16[192,1024]{1,0:T(8,128)(2,1)S(1)}, u32[]{:S(2)}, u32[]{:S(2)}) collective-permute-start(bf16[192,1024]{1,0:T(8,128)(2,1)S(1)} %add_convert_fusion.2.refs_0_), channel_id=1, source_target_pairs={{0,64},{1,65},{2,66},{3,67},{4,68},{5,69},{6,70},{7,71},{8,72},{9,... | collective-permute-start | bytes 1179656 | tf_op jit(solution)/shard_map/ppermute | solution.py:53
  76.9 3.8 %collective-permute-done.9 = bf16[4,384,128]{2,1,0:T(8,128)(2,1)S(1)} collective-permute-done((bf16[4,384,128]{2,1,0:T(8,128)(2,1)S(1)}, bf16[4,384,128]{2,1,0:T(8,128)(2,1)S(1)}, u32[]{:S(2)}, u32[]{:S(2)}) %collective-permute-start.9) | collective-permute-done | bytes 393248 | tf_op jit(solution)/shard_map/ppermute | solution.py:53
  80.7 2.4 %all-gather.2 = bf16[8,384,128]{2,1,0:T(8,128)(2,1)S(1)} all-gather(bf16[4,384,128]{2,1,0:T(8,128)(2,1)S(1)} %collective-permute-done.9), channel_id=4, replica_groups=mesh['xh'=2,'y'=4,'core'=2,'zh'=4,'zl'=4,'xl'=2] {'core'}, dimensions={0}, use_global_device_ids=true | all-gather | bytes 1179648 | tf_op jit(solution)/shard_map/all_gather | solution.py:254
  83.0 3.5 %shard_map.80 = (bf16[128,256]{1,0:T(8,128)(2,1)S(1)}, bf16[128,256]{1,0:T(8,128)(2,1)S(1)}, bf16[128,256]{1,0:T(8,128)(2,1)S(1)}, bf16[128,256]{1,0:T(8,128)(2,1)S(1)}) custom-call(bf16[128,6144]{1,0:T(8,128)(2,1)S(1)} %copy-done, bf16[128,6144]{1,0:T(8,128)(2,1)S(1)} %collective-permute-done.4.refs_0_.refs_1_, ...), custom_call_target="tpu_custom_call" | custom-call | flops 1610612736 | bytes 9437184 | tf_op jit(solution)/shard_map/pallas_call | solution.py:193
  86.8 2.9 %collective-permute-start.10 = (bf16[192,1024]{1,0:T(8,128)(2,1)S(1)}, bf16[192,1024]{1,0:T(8,128)(2,1)S(1)}, u32[]{:S(2)}, u32[]{:S(2)}) collective-permute-start(bf16[192,1024]{1,0:T(8,128)(2,1)S(1)} %add_convert_fusion.1), channel_id=1, source_target_pairs={{0,256},{1,257},{2,258},{3,259},{4,260},{5,261},{6,262},{7,263},{8... | collective-permute-start | bytes 1179656 | tf_op jit(solution)/shard_map/ppermute | solution.py:53
  89.8 1.9 %collective-permute-start.11 = (bf16[128,256]{1,0:T(8,128)(2,1)S(1)}, bf16[128,256]{1,0:T(8,128)(2,1)S(1)}, u32[]{:S(2)}, u32[]{:S(2)}) collective-permute-start(bf16[128,256]{1,0:T(8,128)(2,1)S(1)} %get-tuple-element.13.refs_2_), channel_id=1, source_target_pairs={{0,192},{1,193},{2,194},{3,195},{4,196},{5,197},{6,198},{7,199},{8... | collective-permute-start | bytes 196616 | tf_op jit(solution)/shard_map/ppermute | solution.py:53
  91.8 5.6 %collective-permute-start.12 = (bf16[128,256]{1,0:T(8,128)(2,1)S(1)}, bf16[128,256]{1,0:T(8,128)(2,1)S(1)}, u32[]{:S(2)}, u32[]{:S(2)}) collective-permute-start(bf16[128,256]{1,0:T(8,128)(2,1)S(1)} %get-tuple-element.14.refs_3_), channel_id=1, source_target_pairs={{0,128},{1,129},{2,130},{3,131},{4,132},{5,133},{6,134},{7,135},{8... | collective-permute-start | bytes 196616 | tf_op jit(solution)/shard_map/ppermute | solution.py:53
  97.4 1.9 %collective-permute-start.13 = (bf16[128,256]{1,0:T(8,128)(2,1)S(1)}, bf16[128,256]{1,0:T(8,128)(2,1)S(1)}, u32[]{:S(2)}, u32[]{:S(2)}) collective-permute-start(bf16[128,256]{1,0:T(8,128)(2,1)S(1)} %get-tuple-element.15.refs_4_), channel_id=1, source_target_pairs={{0,64},{1,65},{2,66},{3,67},{4,68},{5,69},{6,70},{7,71},{8,72},{9,... | collective-permute-start | bytes 196616 | tf_op jit(solution)/shard_map/ppermute | solution.py:53
  99.3 2.9 %collective-permute-done.10 = bf16[192,1024]{1,0:T(8,128)(2,1)S(1)} collective-permute-done((bf16[192,1024]{1,0:T(8,128)(2,1)S(1)}, bf16[192,1024]{1,0:T(8,128)(2,1)S(1)}, u32[]{:S(2)}, u32[]{:S(2)}) %collective-permute-start.10) | collective-permute-done | bytes 393248 | tf_op jit(solution)/shard_map/ppermute | solution.py:53
  102.2 2.2 %fusion.4 = (bf16[192,1024]{1,0:T(8,128)(2,1)S(1)}, bf16[1,192,1024]{2,1,0:T(8,128)(2,1)}) fusion(bf16[192,1024]{1,0:T(8,128)(2,1)S(1)} %copy-done.5, bf16[192,1024]{1,0:T(8,128)(2,1)S(1)} %collective-permute-done.10, bf16[192,1024]{1,0:T(8,128)(2,1)S(1)} %add_convert_fusion.1, bf16[1,192,1024]{2,1,0:T(8,128)(2,1)S(1)} %copy-done.4, ...), kind=kLoop, calls=%fused_computation.8 | loop fusion | flops 3932160 | bytes 2752516 | tf_op jit(solution)/shard_map/convert_element_type | solution.py:276
  (31 shorter events, 5.6 us)
Async XLA Ops:
  0.6 10.0 %copy-start = (bf16[128,6144]{1,0:T(8,128)(2,1)S(1)}, bf16[128,6144]{1,0:T(8,128)(2,1)}, u32[]{:S(2)}) copy-start(bf16[128,6144]{1,0:T(8,128)(2,1)} %refs_0_.2) | copy-start | bytes 4718596
  0.6 0.8 copy-start.2
  2.8 10.4 %collective-permute-start.3 = (bf16[192,128]{1,0:T(8,128)(2,1)S(1)}, bf16[192,128]{1,0:T(8,128)(2,1)S(1)}, u32[]{:S(2)}, u32[]{:S(2)}) collective-permute-start(bf16[192,128]{1,0:T(8,128)(2,1)S(1)} %get-tuple-element.11), channel_id=1, source_target_pairs={{0,1},{1,0},{2,3},{3,2},{4,5},{5,4},{6,7},{7,6},{8,9},{9,8},{10,11... | collective-permute-start | bytes 147464 | tf_op jit(solution)/shard_map/ppermute | solution.py:53
  13.2 42.8 %copy-start.4 = (bf16[1,192,1024]{2,1,0:T(8,128)(2,1)S(1)}, bf16[1,192,1024]{2,1,0:T(8,128)(2,1)}, u32[]{:S(2)}) copy-start(bf16[1,192,1024]{2,1,0:T(8,128)(2,1)} %param.7) | copy-start | bytes 1179652
  13.2 56.5 %collective-permute-start.4 = (bf16[128,6144]{1,0:T(8,128)(2,1)S(1)}, bf16[128,6144]{1,0:T(8,128)(2,1)S(1)}, u32[]{:S(2)}, u32[]{:S(2)}) collective-permute-start(bf16[128,6144]{1,0:T(8,128)(2,1)S(1)} %shard_map.77), channel_id=1, source_target_pairs={{0,64},{1,65},{2,66},{3,67},{4,68},{5,69},{6,70},{7,71},{8,72},{9,... | collective-permute-start | bytes 4718600 | tf_op jit(solution)/shard_map/ppermute | solution.py:53
  15.3 54.5 %collective-permute-start.5 = (bf16[128,6144]{1,0:T(8,128)(2,1)S(1)}, bf16[128,6144]{1,0:T(8,128)(2,1)S(1)}, u32[]{:S(2)}, u32[]{:S(2)}) collective-permute-start(bf16[128,6144]{1,0:T(8,128)(2,1)S(1)} %shard_map.77), channel_id=1, source_target_pairs={{0,128},{1,129},{2,130},{3,131},{4,132},{5,133},{6,134},{7,135},{8... | collective-permute-start | bytes 4718600 | tf_op jit(solution)/shard_map/ppermute | solution.py:53
  17.2 52.5 %collective-permute-start.6 = (bf16[128,6144]{1,0:T(8,128)(2,1)S(1)}, bf16[128,6144]{1,0:T(8,128)(2,1)S(1)}, u32[]{:S(2)}, u32[]{:S(2)}) collective-permute-start(bf16[128,6144]{1,0:T(8,128)(2,1)S(1)} %shard_map.77), channel_id=1, source_target_pairs={{0,192},{1,193},{2,194},{3,195},{4,196},{5,197},{6,198},{7,199},{8... | collective-permute-start | bytes 4718600 | tf_op jit(solution)/shard_map/ppermute | solution.py:53
  52.7 15.1 %collective-permute-start.7 = (bf16[2,4,384,128]{3,2,1,0:T(8,128)(2,1)S(1)}, bf16[2,4,384,128]{3,2,1,0:T(8,128)(2,1)S(1)}, u32[]{:S(2)}, u32[]{:S(2)}) collective-permute-start(bf16[2,4,384,128]{3,2,1,0:T(8,128)(2,1)S(1)} %bitcast.15), channel_id=1, source_target_pairs={{0,2},{1,3},{2,4},{3,5},{4,6},{5,7},{6,8},{7,9},{8,10},{9,11},{10,... | collective-permute-start | bytes 2359304 | tf_op jit(solution)/shard_map/ppermute | solution.py:53
  56.0 3.6 %collective-permute-start = (bf16[192,1024]{1,0:T(8,128)(2,1)S(1)}, bf16[192,1024]{1,0:T(8,128)(2,1)S(1)}, u32[]{:S(2)}, u32[]{:S(2)}) collective-permute-start(bf16[192,1024]{1,0:T(8,128)(2,1)S(1)} %bitcast.22), channel_id=1, source_target_pairs={{0,32},{1,33},{2,34},{3,35},{4,36},{5,37},{6,38},{7,39},{8,40},{9,... | collective-permute-start | bytes 1179656 | tf_op jit(solution)/shard_map/ppermute | solution.py:53
  59.7 14.6 %collective-permute-start.1 = (bf16[192,1024]{1,0:T(8,128)(2,1)S(1)}, bf16[192,1024]{1,0:T(8,128)(2,1)S(1)}, u32[]{:S(2)}, u32[]{:S(2)}) collective-permute-start(bf16[192,1024]{1,0:T(8,128)(2,1)S(1)} %fusion), channel_id=1, source_target_pairs={{0,128},{1,129},{2,130},{3,131},{4,132},{5,133},{6,134},{7,135},{8... | collective-permute-start | bytes 1179656 | tf_op jit(solution)/shard_map/ppermute | solution.py:53
  67.8 15.2 %collective-permute-start.8 = (bf16[2,4,384,128]{3,2,1,0:T(8,128)(2,1)S(1)}, bf16[2,4,384,128]{3,2,1,0:T(8,128)(2,1)S(1)}, u32[]{:S(2)}, u32[]{:S(2)}) collective-permute-start(bf16[2,4,384,128]{3,2,1,0:T(8,128)(2,1)S(1)} %collective-permute-done.7.value_ref.refs_5_), channel_id=1, source_target_pairs={{0,32},{1,33},{2,34},{3,35},{4,36},{5,37},{6,38},{7,39},{8,40},{9,... | collective-permute-start | bytes 2359304 | tf_op jit(solution)/shard_map/ppermute | solution.py:53
  69.8 10.9 %collective-permute-start.9 = (bf16[4,384,128]{2,1,0:T(8,128)(2,1)S(1)}, bf16[4,384,128]{2,1,0:T(8,128)(2,1)S(1)}, u32[]{:S(2)}, u32[]{:S(2)}) collective-permute-start(bf16[4,384,128]{2,1,0:T(8,128)(2,1)S(1)} %shard_map.79), channel_id=1, source_target_pairs={{0,2},{1,3},{2,4},{3,5},{4,6},{5,7},{6,8},{7,9},{8,10},{9,11},{10,... | collective-permute-start | bytes 1179656 | tf_op jit(solution)/shard_map/ppermute | solution.py:53
  74.4 12.2 %collective-permute-start.2 = (bf16[192,1024]{1,0:T(8,128)(2,1)S(1)}, bf16[192,1024]{1,0:T(8,128)(2,1)S(1)}, u32[]{:S(2)}, u32[]{:S(2)}) collective-permute-start(bf16[192,1024]{1,0:T(8,128)(2,1)S(1)} %add_convert_fusion.2.refs_0_), channel_id=1, source_target_pairs={{0,64},{1,65},{2,66},{3,67},{4,68},{5,69},{6,70},{7,71},{8,72},{9,... | collective-permute-start | bytes 1179656 | tf_op jit(solution)/shard_map/ppermute | solution.py:53
  86.6 3.1 %copy-start.3 = (s32[6]{0:T(128)S(1)}, s32[6]{0:T(128)}, u32[]{:S(2)}) copy-start(s32[6]{0:T(128)} %fragment_ref.1) | copy-start | bytes 76
  86.6 15.6 %copy-start.5 = (bf16[192,1024]{1,0:T(8,128)(2,1)S(1)}, bf16[192,1024]{1,0:T(8,128)(2,1)}, u32[]{:S(2)}) copy-start(bf16[192,1024]{1,0:T(8,128)(2,1)} %param.6) | copy-start | bytes 1179652
  86.8 15.4 %collective-permute-start.10 = (bf16[192,1024]{1,0:T(8,128)(2,1)S(1)}, bf16[192,1024]{1,0:T(8,128)(2,1)S(1)}, u32[]{:S(2)}, u32[]{:S(2)}) collective-permute-start(bf16[192,1024]{1,0:T(8,128)(2,1)S(1)} %add_convert_fusion.1), channel_id=1, source_target_pairs={{0,256},{1,257},{2,258},{3,259},{4,260},{5,261},{6,262},{7,263},{8... | collective-permute-start | bytes 1179656 | tf_op jit(solution)/shard_map/ppermute | solution.py:53
  89.8 14.6 %collective-permute-start.11 = (bf16[128,256]{1,0:T(8,128)(2,1)S(1)}, bf16[128,256]{1,0:T(8,128)(2,1)S(1)}, u32[]{:S(2)}, u32[]{:S(2)}) collective-permute-start(bf16[128,256]{1,0:T(8,128)(2,1)S(1)} %get-tuple-element.13.refs_2_), channel_id=1, source_target_pairs={{0,192},{1,193},{2,194},{3,195},{4,196},{5,197},{6,198},{7,199},{8... | collective-permute-start | bytes 196616 | tf_op jit(solution)/shard_map/ppermute | solution.py:53
  91.8 12.6 %collective-permute-start.12 = (bf16[128,256]{1,0:T(8,128)(2,1)S(1)}, bf16[128,256]{1,0:T(8,128)(2,1)S(1)}, u32[]{:S(2)}, u32[]{:S(2)}) collective-permute-start(bf16[128,256]{1,0:T(8,128)(2,1)S(1)} %get-tuple-element.14.refs_3_), channel_id=1, source_target_pairs={{0,128},{1,129},{2,130},{3,131},{4,132},{5,133},{6,134},{7,135},{8... | collective-permute-start | bytes 196616 | tf_op jit(solution)/shard_map/ppermute | solution.py:53
  97.4 7.4 %collective-permute-start.13 = (bf16[128,256]{1,0:T(8,128)(2,1)S(1)}, bf16[128,256]{1,0:T(8,128)(2,1)S(1)}, u32[]{:S(2)}, u32[]{:S(2)}) collective-permute-start(bf16[128,256]{1,0:T(8,128)(2,1)S(1)} %get-tuple-element.15.refs_4_), channel_id=1, source_target_pairs={{0,64},{1,65},{2,66},{3,67},{4,68},{5,69},{6,70},{7,71},{8,72},{9,... | collective-permute-start | bytes 196616 | tf_op jit(solution)/shard_map/ppermute | solution.py:53
  104.4 1.1 %copy-start.1 = (bf16[192,1024]{1,0:T(8,128)(2,1)}, bf16[192,1024]{1,0:T(8,128)(2,1)S(1)}, u32[]{:S(2)}) copy-start(bf16[192,1024]{1,0:T(8,128)(2,1)S(1)} %get-tuple-element.19.refs_4_) | copy-start | bytes 1179652
